TPU v7x, 32 devices: a whole 2x2x4 slice. The times are simulated.
32 devices in a mesh: section: 2 (over core), rows: 16 (over z, y, x).
Axes of the slice: x: 2, y: 2, z: 4, core: 2. Of those that a mesh axis runs over, the one named last changes fastest.
Arguments:
- tokens: bfloat16 [4096, 768], P('rows'), may hold values from -6 to 6
- segment_ids: int32 [4096], P('rows'), may hold values from 0 to 127, never falling along the last dimension, each value on 1 to 128 neighbouring positions
- in_proj: bfloat16 [2, 2, 768, 3072], P('section'), may hold values from -0.21875 to 0.21875
- out_proj: bfloat16 [2, 3072, 768], replicated, may hold values from -0.109375 to 0.109375
- front_gain: float32 [2, 2, 768], replicated, may hold values from 0.1 to 1.9
- mixer_gain: float32 [2, 768], replicated, may hold values from 0.1 to 1.9
- feed_gain: float32 [2, 3072], replicated, may hold values from 0.1 to 1.9
- cotangent: bfloat16 [4096, 768], P('rows'), may hold values from -6 to 6
Outputs:
- layer_out: bfloat16 [4096, 768], P('rows')
- input_grad: bfloat16 [4096, 768], P('rows')
- grad_in_proj: float32 [2, 2, 768, 3072], P('section', None, None, 'rows')
- grad_out_proj: float32 [2, 3072, 768], P(None, 'rows', 'section')
- grad_front_gain: float32 [2, 2, 768], replicated
- grad_mixer_gain: float32 [2, 768], replicated
- grad_feed_gain: float32 [2, 3072], replicated
All inputs are finite; a program needn't handle non-finite values.
Results may differ from a plain program's by a relative error of at most 0.02.
Values may be sent and summed in bfloat16 or wider, within the bound.
A program may use at most 320 MiB of HBM per device.

v0:
```python
import jax
import jax.numpy as jnp
from jax import lax
from jax.sharding import PartitionSpec as P

HEAD_DIM = 64
SEQ = 128


EPSILON = 1e-05


def passed_along(array, axis, by):
    devices = lax.axis_size(axis)
    pairs = [(i, i + by) for i in range(devices) if 0 <= i + by < devices]
    return lax.ppermute(array, axis, pairs)


def layer_norm(values, gain):
    centered = values - jnp.mean(values, axis=-1, keepdims=True)
    spread = jnp.mean(centered * centered, axis=-1, keepdims=True)
    return centered * lax.rsqrt(spread + EPSILON) * gain


def gelu_exact(values):
    return jax.nn.gelu(values, approximate=False)


def visible(segment, seq_count):
    segment_grid = segment.reshape(seq_count, SEQ)
    position = jnp.arange(SEQ)
    causal = position[:, None] >= position[None, :]
    same_doc = segment_grid[:, :, None] == segment_grid[:, None, :]
    return jnp.logical_and(causal[None], same_doc)


def attention_forward(stream, segment, weight, gain_in, gain_mid):
    model_width = stream.shape[1]
    seq_count = stream.shape[0] // SEQ
    head_count = model_width // HEAD_DIM
    normed = layer_norm(stream, gain_in).astype(jnp.bfloat16)
    projected = jnp.dot(
        normed, weight[:, : 3 * model_width], preferred_element_type=jnp.float32
    ).astype(jnp.bfloat16)
    shaped = projected.reshape(seq_count, SEQ, 3, head_count, HEAD_DIM)
    queries = shaped[:, :, 0]
    key_rows = shaped[:, :, 1]
    value_rows = shaped[:, :, 2]
    scores = jnp.einsum(
        "bqhd,bkhd->bhqk", queries, key_rows, preferred_element_type=jnp.float32
    ) * HEAD_DIM ** (-0.5)
    allowed = visible(segment, seq_count)
    scores = jnp.where(allowed[:, None], scores, -1e30)
    row_peak = jnp.max(scores, axis=-1, keepdims=True)
    weights = jnp.exp(scores - row_peak)
    attention = weights / jnp.sum(weights, axis=-1, keepdims=True)
    attention_low = attention.astype(jnp.bfloat16)
    context = jnp.einsum(
        "bhqk,bkhd->bqhd", attention_low, value_rows, preferred_element_type=jnp.float32
    )
    context = context.reshape(-1, model_width)
    inner_normed = layer_norm(context, gain_mid).astype(jnp.bfloat16)
    branch = jnp.dot(
        inner_normed, weight[:, 3 * model_width :], preferred_element_type=jnp.float32
    ).astype(jnp.bfloat16)
    return (
        branch,
        (normed, queries, key_rows, value_rows, attention, attention_low, context, inner_normed),
    )


def attention_backward(stream, segment, weight, gain_in, gain_mid, upstream):
    model_width = stream.shape[1]
    seq_count = stream.shape[0] // SEQ
    head_count = model_width // HEAD_DIM
    scale = HEAD_DIM ** (-0.5)
    branch, kept = attention_forward(stream, segment, weight, gain_in, gain_mid)
    normed, queries, key_rows, value_rows, attention, attention_low, context, inner_normed = kept
    branch_grad = upstream.astype(jnp.bfloat16)
    out_weight_grad = jnp.einsum(
        "tc,td->cd", inner_normed, branch_grad, preferred_element_type=jnp.float32
    )
    inner_grad = jnp.einsum(
        "td,cd->tc", branch_grad, weight[:, 3 * model_width :], preferred_element_type=jnp.float32
    )
    unused_value, mid_pull = jax.vjp(layer_norm, context, gain_mid)
    context_grad, mid_gain_grad = mid_pull(inner_grad)
    context_low = context_grad.astype(jnp.bfloat16).reshape(seq_count, SEQ, head_count, HEAD_DIM)
    prob_grad = jnp.einsum(
        "bqhd,bkhd->bhqk", context_low, value_rows, preferred_element_type=jnp.float32
    )
    value_grad = jnp.einsum(
        "bhqk,bqhd->bkhd", attention_low, context_low, preferred_element_type=jnp.float32
    )
    score_grad = attention * (prob_grad - jnp.sum(attention * prob_grad, axis=-1, keepdims=True))
    score_low = score_grad.astype(jnp.bfloat16)
    query_grad = (
        jnp.einsum("bhqk,bkhd->bqhd", score_low, key_rows, preferred_element_type=jnp.float32)
        * scale
    )
    key_grad = (
        jnp.einsum("bhqk,bqhd->bkhd", score_low, queries, preferred_element_type=jnp.float32)
        * scale
    )
    projected_grad = jnp.stack([query_grad, key_grad, value_grad], axis=2).astype(jnp.bfloat16)
    projected_grad = projected_grad.reshape(-1, 3 * model_width)
    in_weight_grad = jnp.einsum(
        "tc,td->cd", normed, projected_grad, preferred_element_type=jnp.float32
    )
    normed_grad = jnp.einsum(
        "td,cd->tc",
        projected_grad,
        weight[:, : 3 * model_width],
        preferred_element_type=jnp.float32,
    )
    unused_front, front_pull = jax.vjp(layer_norm, stream, gain_in)
    stream_grad, front_gain_grad = front_pull(normed_grad)
    weight_grad = jnp.concatenate([in_weight_grad, out_weight_grad], axis=1)
    return (stream_grad.astype(jnp.bfloat16), weight_grad, front_gain_grad, mid_gain_grad)


def feed_forward(stream, weight_in, weight_out, gain_in, gain_mid):
    normed = layer_norm(stream, gain_in).astype(jnp.bfloat16)
    hidden = jnp.dot(normed, weight_in, preferred_element_type=jnp.float32)
    activated = gelu_exact(hidden)
    inner_normed = layer_norm(activated, gain_mid).astype(jnp.bfloat16)
    branch = jnp.dot(inner_normed, weight_out, preferred_element_type=jnp.float32).astype(
        jnp.bfloat16
    )
    return (branch, (normed, hidden, activated, inner_normed))


def feed_backward(stream, weight_in, weight_out, gain_in, gain_mid, upstream):
    branch, kept = feed_forward(stream, weight_in, weight_out, gain_in, gain_mid)
    normed, hidden, activated, inner_normed = kept
    branch_grad = upstream.astype(jnp.bfloat16)
    out_weight_grad = jnp.einsum(
        "tc,td->cd", inner_normed, branch_grad, preferred_element_type=jnp.float32
    )
    inner_grad = jnp.einsum(
        "td,cd->tc", branch_grad, weight_out, preferred_element_type=jnp.float32
    )
    unused_value, mid_pull = jax.vjp(layer_norm, activated, gain_mid)
    act_grad, mid_gain_grad = mid_pull(inner_grad)
    unused_act, gelu_pull = jax.vjp(gelu_exact, hidden)
    hidden_grad = gelu_pull(act_grad)[0].astype(jnp.bfloat16)
    in_weight_grad = jnp.einsum(
        "tc,td->cd", normed, hidden_grad, preferred_element_type=jnp.float32
    )
    normed_grad = jnp.einsum(
        "td,cd->tc", hidden_grad, weight_in, preferred_element_type=jnp.float32
    )
    unused_front, front_pull = jax.vjp(layer_norm, stream, gain_in)
    stream_grad, front_gain_grad = front_pull(normed_grad)
    return (
        stream_grad.astype(jnp.bfloat16),
        in_weight_grad,
        out_weight_grad,
        front_gain_grad,
        mid_gain_grad,
    )


def accumulate(store, label, value):
    if label in store:
        store[label] = store[label] + value
    else:
        store[label] = value


def local(tokens, segment_ids, in_proj, out_proj, front_gain, mixer_gain, feed_gain, cotangent):
    own_section = lax.axis_index("section")
    own_weights = in_proj[0]
    layer_total = own_weights.shape[0]
    model_width = front_gain.shape[2]
    hidden_width = feed_gain.shape[1]
    in_store = {}
    out_store = {}
    front_store = {}
    mixer_store = {}
    feed_store = {}

    def run_forward(sublayer, layer_index, stream, segment):
        if sublayer == 0:
            return attention_forward(
                stream,
                segment,
                own_weights[layer_index],
                front_gain[layer_index, 0],
                mixer_gain[layer_index],
            )[0]
        return feed_forward(
            stream,
            own_weights[layer_index],
            out_proj[layer_index],
            front_gain[layer_index, 1],
            feed_gain[layer_index],
        )[0]

    def resting_grads(stream):
        return (
            jnp.zeros(stream.shape, jnp.bfloat16),
            jnp.zeros(own_weights.shape[1:], jnp.float32),
            jnp.zeros(out_proj.shape[1:], jnp.float32),
            jnp.zeros((model_width,), jnp.float32),
            jnp.zeros((model_width,), jnp.float32),
            jnp.zeros((hidden_width,), jnp.float32),
        )

    def run_backward(sublayer, layer_index, stream, segment, upstream):
        if sublayer == 0:
            stream_grad, weight_grad, front_grad, mid_grad = attention_backward(
                stream,
                segment,
                own_weights[layer_index],
                front_gain[layer_index, 0],
                mixer_gain[layer_index],
                upstream,
            )
            return (
                stream_grad,
                weight_grad,
                jnp.zeros(out_proj.shape[1:], jnp.float32),
                front_grad,
                mid_grad,
                jnp.zeros((hidden_width,), jnp.float32),
            )
        stream_grad, in_grad, out_grad, front_grad, mid_grad = feed_backward(
            stream,
            own_weights[layer_index],
            out_proj[layer_index],
            front_gain[layer_index, 1],
            feed_gain[layer_index],
            upstream,
        )
        return (
            stream_grad,
            in_grad,
            out_grad,
            front_grad,
            jnp.zeros((model_width,), jnp.float32),
            mid_grad,
        )

    stream = tokens.astype(jnp.float32)
    upstream = cotangent.astype(jnp.float32)
    kept_streams = []
    for layer_index in range(layer_total):
        for sublayer in (0, 1):
            kept_streams.append(stream)

            def active_forward(stream_in):
                return run_forward(sublayer, layer_index, stream_in, segment_ids)

            def resting_forward(stream_in):
                return jnp.zeros(stream_in.shape, jnp.bfloat16)

            own_branch = lax.cond(own_section == sublayer, active_forward, resting_forward, stream)
            if sublayer == 0:
                received = passed_along(own_branch, "section", 1)
            else:
                received = passed_along(own_branch, "section", -1)
            stream = stream + jnp.where(own_section == sublayer, own_branch, received).astype(
                jnp.float32
            )
    for position in reversed(range(2 * layer_total)):
        layer_index, sublayer = divmod(position, 2)

        def active_backward(operand):
            return run_backward(sublayer, layer_index, operand[0], segment_ids, operand[1])

        def resting_backward(operand):
            return resting_grads(operand[0])

        grads = lax.cond(
            own_section == sublayer,
            active_backward,
            resting_backward,
            (kept_streams[position], upstream),
        )
        own_grad = grads[0]
        accumulate(in_store, layer_index, grads[1])
        accumulate(out_store, layer_index, grads[2])
        accumulate(front_store, (layer_index, sublayer), grads[3])
        accumulate(mixer_store, layer_index, grads[4])
        accumulate(feed_store, layer_index, grads[5])
        if sublayer == 0:
            received = passed_along(own_grad, "section", 1)
        else:
            received = passed_along(own_grad, "section", -1)
        upstream = upstream + jnp.where(own_section == sublayer, own_grad, received).astype(
            jnp.float32
        )
    in_total = jnp.stack([in_store[layer_index] for layer_index in range(layer_total)])
    out_total = jnp.stack([out_store[layer_index] for layer_index in range(layer_total)])
    front_total = jnp.stack(
        [
            jnp.stack([front_store[layer_index, 0], front_store[layer_index, 1]])
            for layer_index in range(layer_total)
        ]
    )
    mixer_total = jnp.stack([mixer_store[layer_index] for layer_index in range(layer_total)])
    feed_total = jnp.stack([feed_store[layer_index] for layer_index in range(layer_total)])
    first_grad = lax.psum_scatter(in_total[None], "rows", scatter_dimension=3, tiled=True)
    partial_sum = lax.psum_scatter(
        out_total.astype(jnp.bfloat16), "section", scatter_dimension=2, tiled=True
    ).astype(jnp.float32)
    second_grad = lax.psum_scatter(partial_sum, "rows", scatter_dimension=1, tiled=True)
    gain_totals = lax.psum((front_total, mixer_total, feed_total), ("section", "rows"))
    return (
        stream.astype(jnp.bfloat16),
        upstream.astype(jnp.bfloat16),
        first_grad,
        second_grad,
        gain_totals[0],
        gain_totals[1],
        gain_totals[2],
    )


def solution(mesh):
    return jax.shard_map(
        local,
        mesh=mesh,
        in_specs=(
            P("rows", None),
            P("rows"),
            P("section", None, None, None),
            P(),
            P(),
            P(),
            P(),
            P("rows", None),
        ),
        out_specs=(
            P("rows", None),
            P("rows", None),
            P("section", None, None, "rows"),
            P(None, "rows", "section"),
            P(),
            P(),
            P(),
        ),
        check_vma=False,
    )
```

profile of v0, /device:TPU:0, one launch (start us, length us, event | category | flops | bytes accessed | tf_op | source)
XLA Modules:
  0.0 835.1 jit_solution(5404306521603937352)
XLA Ops:
  9.2 20.8 %conditional.8 = (bf16[256,768]{1,0:T(8,128)(2,1)S(1)}) conditional(s32[]{:T(128)} %convert_element_type.217, () %tuple.100, (f32[256,768]{1,0:T(8,128)}, f32[2,2,768]{2,1,0:T(2,128)}, bf16[2,768,3072]{2,1,0:T(8,128)(2,1)}, s32[256]{0:T(256)}, f32[2,768]{1,0:T(2,128)}) %tuple.204), branch_computations={%region_0.0_spmd, %region_1.8_spmd} | conditional | flops 1314996864 | bytes 52460584 | solution.py:258
  14.2 2.7 slice_bitcast_fusion
  18.9 2.3 convolution_convert_fusion
  34.3 14.7 %collective-permute-done.1 = bf16[256,768]{1,0:T(8,128)(2,1)S(1)} collective-permute-done((bf16[256,768]{1,0:T(8,128)(2,1)S(1)}, bf16[256,768]{1,0:T(8,128)(2,1)S(1)}, u32[]{:S(2)}, u32[]{:S(2)}) %collective-permute-start.1) | collective-permute-done | bytes 393248 | tf_op jit(solution)/shard_map/ppermute | solution.py:16
  49.2 22.1 %conditional.10 = (bf16[256,768]{1,0:T(8,128)(2,1)S(1)}) conditional(s32[]{:T(128)} %convert_element_type.217, () %tuple.104, (f32[256,768]{1,0:T(8,128)S(1)}, f32[2,2,768]{2,1,0:T(2,128)}, bf16[2,768,3072]{2,1,0:T(8,128)(2,1)}, s32[256]{0:T(256)S(1)}, f32[2,768]{1,0:T(2,128)}) %tuple.215), branch_computations={%region_14.15_spmd, %region_15.22_spmd} | conditional | flops 1314996864 | bytes 52460584 | solution.py:258
  51.7 2.7 slice_bitcast_fusion.1
  59.1 2.8 reshape.550
  63.9 3.0 fusion.225
  74.9 12.2 %conditional.12 = (bf16[256,768]{1,0:T(8,128)(2,1)S(1)}, f32[3072,768]{1,0:T(8,128)}, f32[3072]{0:T(1024)S(1)}, f32[]{:T(128)}, f32[1,768]{1,0:T(1,128)S(1)}, /*index=5*/f32[768,3072]{0,1:T(8,128)}) conditional(s32[]{:T(128)} %convert_element_type.219, () %tuple.108, (f32[256,768]{1,0:T(8,128)S(1)}, f32[2,2,768]{2,1,0:T(2,128)}, ...), branch_computations={%region_28.29_spmd, %region_29.40_spmd} | conditional | flops 6128663552 | bytes 141375728 | solution.py:275
  74.9 4.2 broadcast.1092
  79.1 4.3 broadcast.1091.clone
  89.0 20.7 %collective-permute-done.4 = bf16[256,768]{1,0:T(8,128)(2,1)S(1)} collective-permute-done((bf16[256,768]{1,0:T(8,128)(2,1)S(1)}, bf16[256,768]{1,0:T(8,128)(2,1)S(1)}, u32[]{:S(2)}, u32[]{:S(2)}) %collective-permute-start.4) | collective-permute-done | bytes 393248 | tf_op jit(solution)/shard_map/ppermute | solution.py:16
  109.8 63.2 %conditional.13 = (bf16[256,768]{1,0:T(8,128)(2,1)S(1)}, f32[768]{0:T(1024)S(1)}, f32[]{:T(128)}, f32[1,768]{1,0:T(1,128)}, f32[768,3072]{0,1:T(8,128)}) conditional(s32[]{:T(128)} %convert_element_type.217, () %tuple.110, (f32[256,768]{1,0:T(8,128)S(1)}, f32[2,2,768]{2,1,0:T(2,128)}, bf16[2,768,3072]{2,1,0:T(8,128)(2,1)}, s32[256]{0:T(256)S(1)}, ...), branch_computations={%region_40.41_spmd, %region_41.55_spmd} | conditional | flops 3645586688 | bytes 170688160 | solution.py:275
  112.9 2.7 slice_bitcast_fusion.2
  120.4 2.9 reshape.552
  125.2 3.0 fusion.229
  133.1 2.5 multiply_reduce_fusion.16
  150.4 4.1 fusion.126
  154.5 8.7 %pad_maximum_fusion = f32[768,3072]{1,0:T(8,128)} fusion(f32[768,768]{1,0:T(8,128)} %fusion.133, f32[768,2304]{1,0:T(8,128)} %fusion.126), kind=kLoop, calls=%fused_computation.215 | loop fusion | flops 2359296 | bytes 18874368 | tf_op jit(solution)/shard_map/cond/branch_1_fun/concatenate | solution.py:118
  163.2 9.6 %copy.158 = f32[768,3072]{0,1:T(8,128)} copy(f32[768,3072]{1,0:T(8,128)} %pad_maximum_fusion) | data formatting | bytes 18874368 | tf_op jit(solution)/shard_map/cond | solution.py:275
  176.4 12.7 %conditional.14 = (bf16[256,768]{1,0:T(8,128)(2,1)S(1)}, f32[3072,768]{1,0:T(8,128)}, f32[3072]{0:T(1024)S(1)}, f32[]{:T(128)}, f32[1,768]{1,0:T(1,128)S(1)}, /*index=5*/f32[768,3072]{0,1:T(8,128)}) conditional(s32[]{:T(128)} %convert_element_type.219, () %tuple.112, (f32[256,768]{1,0:T(8,128)S(1)}, f32[2,2,768]{2,1,0:T(2,128)}, ...), branch_computations={%region_55.56_spmd, %region_56.67_spmd} | conditional | flops 6129056768 | bytes 142162160 | solution.py:275
  176.4 4.2 broadcast.1141
  180.7 4.2 broadcast.1140.clone
  191.0 6.5 fusion.209
  197.5 13.8 %collective-permute-done.6 = bf16[256,768]{1,0:T(8,128)(2,1)S(1)} collective-permute-done((bf16[256,768]{1,0:T(8,128)(2,1)S(1)}, bf16[256,768]{1,0:T(8,128)(2,1)S(1)}, u32[]{:S(2)}, u32[]{:S(2)}) %collective-permute-start.6) | collective-permute-done | bytes 393248 | tf_op jit(solution)/shard_map/ppermute | solution.py:16
  211.4 61.1 %conditional.15 = (bf16[256,768]{1,0:T(8,128)(2,1)}, f32[768]{0:T(1024)}, f32[]{:T(128)}, f32[1,768]{1,0:T(1,128)}, f32[768,3072]{0,1:T(8,128)}) conditional(s32[]{:T(128)} %convert_element_type.217, () %tuple.114, (f32[256,768]{1,0:T(8,128)}, f32[2,2,768]{2,1,0:T(2,128)}, bf16[2,768,3072]{2,1,0:T(8,128)(2,1)}, s32[256]{0:T(256)S(1)}, ...), branch_computations={%region_67.68_spmd, %region_68.82_spmd} | conditional | flops 3645586688 | bytes 173813216 | solution.py:275
  215.5 2.7 slice_bitcast_fusion.3
  220.4 2.3 convolution_convert_fusion.6
  224.1 2.9 reshape.555
  233.3 2.5 multiply_reduce_fusion.29
  244.0 2.5 multiply_reduce_fusion.28
  249.4 5.5 fusion.185
  254.9 7.9 pad_maximum_fusion.2
  262.9 9.5 %copy.162 = f32[768,3072]{0,1:T(8,128)} copy(f32[768,3072]{1,0:T(8,128)} %pad_maximum_fusion.2) | data formatting | bytes 18874368 | tf_op jit(solution)/shard_map/cond | solution.py:275
  272.6 6.6 fusion.208
  279.2 8.3 pad_maximum_fusion.4
  287.4 24.0 %copy.153 = bf16[2,3072,768]{1,0,2:T(2,128)(2,1)} copy(bf16[2,3072,768]{2,1,0:T(8,128)(2,1)} %pad_maximum_fusion.4) | data formatting | bytes 18874368
  311.5 10.4 %copy.185 = bf16[96,8,2,3072]{3,1,2,0:T(8,128)(2,1)} copy(bf16[96,8,2,3072]{3,2,1,0:T(2,128)(2,1)} %bitcast.346) | data formatting | bytes 18874368
  321.9 12.6 %add_bitcast_fusion = f32[1,768,3072]{1,2,0:T(8,128)} fusion(f32[768,3072]{0,1:T(8,128)} %get-tuple-element.293, f32[768,3072]{0,1:T(8,128)} %get-tuple-element.294), kind=kLoop, calls=%fused_computation.426 | loop fusion | flops 2359296 | bytes 28311552 | tf_op jit(solution)/shard_map/stack | solution.py:294
  334.5 14.1 %add_bitcast_fusion.1 = f32[1,768,3072]{1,2,0:T(8,128)} fusion(f32[768,3072]{0,1:T(8,128)} %get-tuple-element.295, f32[768,3072]{0,1:T(8,128)} %get-tuple-element.296), kind=kLoop, calls=%fused_computation.427 | loop fusion | flops 2359296 | bytes 28311552 | tf_op jit(solution)/shard_map/stack | solution.py:294
  348.6 14.7 %maximum_bitcast_fusion = f32[1,2,768,3072]{2,3,1,0:T(8,128)} fusion(f32[1,768,3072]{1,2,0:T(8,128)} %add_bitcast_fusion, f32[1,768,3072]{1,2,0:T(8,128)} %add_bitcast_fusion.1), kind=kLoop, calls=%fused_computation.422 | loop fusion | flops 4718592 | bytes 37748736 | tf_op jit(solution)/shard_map/broadcast_in_dim | solution.py:304
  363.3 8.3 reshape.559
  371.6 12.6 %copy.154 = bf16[2,3072,384]{2,1,0:T(8,128)(2,1)} copy(bf16[2,3072,384]{1,0,2:T(2,128)(2,1)} %bitcast.347) | data formatting | bytes 9437184
  384.2 6.6 convert_element_type.230
  393.7 2.2 collective-permute-done.3
  400.3 44.7 %all-reduce = (f32[2,2,768]{2,1,0:T(2,128)}, f32[2,768]{1,0:T(2,128)}, f32[2,3072]{1,0:T(2,128)}) all-reduce(f32[2,2,768]{2,1,0:T(2,128)S(1)} %pad_maximum_fusion.6, f32[2,768]{1,0:T(2,128)S(1)} %pad_maximum_fusion.7, f32[2,3072]{1,0:T(2,128)S(1)} %pad_maximum_fusion.5), channel_id=1, replica_groups=mesh['section'=2,'rows'=16] {'section','rows'}, use_global_device_ids=true, to_apply=%region_85.86 | all-reduce | flops 10752 | bytes 86016 | tf_op jit(solution)/shard_map/psum | solution.py:309
  446.9 204.7 %reduce-scatter.6.cloned.1.call-done = f32[1,2,768,192]{2,3,1,0:T(8,128)} async-done(((f32[1,2,768,3072]{2,3,1,0:T(8,128)}), f32[1,2,768,192]{2,3,1,0:T(8,128)}) %reduce-scatter.6.cloned.1.call-update) | async-done | bytes 1179664 | tf_op jit(solution)/shard_map/reduce_scatter | solution.py:304
  651.6 176.6 %reduce-scatter.8.cloned.1.call-done = f32[2,192,384]{2,1,0:T(8,128)} async-done(((f32[2,3072,384]{2,1,0:T(8,128)}), f32[2,192,384]{2,1,0:T(8,128)}) %reduce-scatter.8.cloned.1.call-update) | async-done | bytes 589840 | tf_op jit(solution)/shard_map/reduce_scatter | solution.py:308
  (275 shorter events, 109.9 us)
Async XLA Ops:
  7.2 356.2 %reduce-scatter.10.cloned.1.call-start = ((), (), s32[]{:S(2)}) async-start(), calls=%async_computation.5 | async-start | bytes 14155776
  9.2 23.4 %copy-start.12 = (bf16[256,768]{1,0:T(8,128)(2,1)S(1)}, bf16[256,768]{1,0:T(8,128)(2,1)}, u32[]{:S(2)}) copy-start(bf16[256,768]{1,0:T(8,128)(2,1)} %param.24) | copy-start | bytes 1179652
  9.2 23.6 %copy-start.19 = (f32[2,3072]{1,0:T(2,128)S(1)}, f32[2,3072]{1,0:T(2,128)}, u32[]{:S(2)}) copy-start(f32[2,3072]{1,0:T(2,128)} %param.30) | copy-start | bytes 73732
  16.8 2.1 copy-start.5
  30.0 2.6 collective-permute-start
  32.7 16.4 %copy-start.21 = (s32[256]{0:T(256)S(1)}, s32[256]{0:T(256)}, u32[]{:S(2)}) copy-start(s32[256]{0:T(256)} %param.25) | copy-start | bytes 3076
  32.8 16.2 %collective-permute-start.1 = (bf16[256,768]{1,0:T(8,128)(2,1)S(1)}, bf16[256,768]{1,0:T(8,128)(2,1)S(1)}, u32[]{:S(2)}, u32[]{:S(2)}) collective-permute-start(bf16[256,768]{1,0:T(8,128)(2,1)S(1)} %get-tuple-element.441), channel_id=1, source_target_pairs={{16,0},{17,1},{18,2},{19,3},{20,4},{21,5},{22,6},{23,7},{24,8},{25... | collective-permute-start | bytes 1179656 | tf_op jit(solution)/shard_map/ppermute | solution.py:16
  49.2 24.9 %copy-start.13 = (bf16[256,768]{1,0:T(8,128)(2,1)S(1)}, bf16[256,768]{1,0:T(8,128)(2,1)}, u32[]{:S(2)}) copy-start(bf16[256,768]{1,0:T(8,128)(2,1)} %param.31) | copy-start | bytes 1179652
  54.4 2.1 copy-start.6
  71.3 2.6 collective-permute-start.2
  87.7 22.1 %copy-start.46 = (f32[1,768]{1,0:T(1,128)}, f32[1,768]{1,0:T(1,128)S(1)}, u32[]{:S(2)}) copy-start(f32[1,768]{1,0:T(1,128)S(1)} %get-tuple-element.286) | copy-start | bytes 9220
  87.7 22.0 %collective-permute-start.4 = (bf16[256,768]{1,0:T(8,128)(2,1)S(1)}, bf16[256,768]{1,0:T(8,128)(2,1)S(1)}, u32[]{:S(2)}, u32[]{:S(2)}) collective-permute-start(bf16[256,768]{1,0:T(8,128)(2,1)S(1)} %get-tuple-element.271), channel_id=1, source_target_pairs={{16,0},{17,1},{18,2},{19,3},{20,4},{21,5},{22,6},{23,7},{24,8},{25... | collective-permute-start | bytes 1179656 | tf_op jit(solution)/shard_map/ppermute | solution.py:16
  110.8 4.8 copy-start.33
  115.6 2.2 copy-start.3
  125.2 3.0 copy-start.14
  130.0 5.6 copy-start.40
  133.1 2.9 copy-start.42
  138.9 2.1 copy-start.41
  138.9 2.1 copy-start.43
  141.0 2.1 copy-start.10
  141.0 2.1 copy-start.15
  141.0 2.1 copy-start.18
  143.1 4.1 slice-start.6
  143.6 3.6 slice-start.7
  163.2 9.6 %copy-start.9 = (bf16[256,768]{1,0:T(8,128)(2,1)S(1)}, bf16[256,768]{1,0:T(8,128)(2,1)}, u32[]{:S(2)}) copy-start(bf16[256,768]{1,0:T(8,128)(2,1)} %add_convert_fusion.2) | copy-start | bytes 1179652 | tf_op jit(solution)/shard_map/cond
  163.2 9.6 %copy-start.37 = (f32[768]{0:T(1024)S(1)}, f32[768]{0:T(1024)}, u32[]{:S(2)}) copy-start(f32[768]{0:T(1024)} %get-tuple-element.414) | copy-start | bytes 9220 | tf_op jit(solution)/shard_map/cond
  173.7 2.6 collective-permute-start.5
  189.7 7.8 copy-start.48
  189.7 21.6 %collective-permute-start.6 = (bf16[256,768]{1,0:T(8,128)(2,1)S(1)}, bf16[256,768]{1,0:T(8,128)(2,1)S(1)}, u32[]{:S(2)}, u32[]{:S(2)}) collective-permute-start(bf16[256,768]{1,0:T(8,128)(2,1)S(1)} %get-tuple-element.273), channel_id=1, source_target_pairs={{16,0},{17,1},{18,2},{19,3},{20,4},{21,5},{22,6},{23,7},{24,8},{25... | collective-permute-start | bytes 1179656 | tf_op jit(solution)/shard_map/ppermute | solution.py:16
  191.0 20.4 %copy-start.28 = (f32[2,768]{1,0:T(2,128)S(1)}, f32[2,768]{1,0:T(2,128)}, u32[]{:S(2)}) copy-start(f32[2,768]{1,0:T(2,128)} %param.29) | copy-start | bytes 18436
  214.6 3.5 copy-start.35
  218.2 2.2 copy-start.4
  228.5 3.6 copy-start.16
  233.2 2.9 copy-start.44
  236.5 2.1 copy-start.45
  238.6 2.1 copy-start.11
  238.6 2.1 copy-start.17
  238.6 2.1 copy-start.32
  240.7 3.2 slice-start.8
  241.2 2.8 slice-start.9
  244.0 3.1 copy-start.54
  249.4 5.5 copy-start.2
  321.9 329.7 %reduce-scatter.6.cloned.1.call-start = ((), (), s32[]{:S(2)}) async-start(), calls=%async_computation.3 | async-start | bytes 20054016 | tf_op jit(solution)/shard_map/reduce_scatter | solution.py:304
  363.3 464.9 %reduce-scatter.8.cloned.1.call-start = ((), (), s32[]{:S(2)}) async-start(), calls=%async_computation.4 | async-start | bytes 10027008 | tf_op jit(solution)/shard_map/reduce_scatter | solution.py:308
  391.9 7.6 copy-start.49
  391.9 8.3 copy-start.27
  392.3 3.6 collective-permute-start.3
  397.4 47.6 %collective-permute-start.7 = (bf16[256,768]{1,0:T(8,128)(2,1)}, bf16[256,768]{1,0:T(8,128)(2,1)S(1)}, u32[]{:S(2)}, u32[]{:S(2)}) collective-permute-start(bf16[256,768]{1,0:T(8,128)(2,1)} %get-tuple-element.274), channel_id=1, source_target_pairs={{0,16},{1,17},{2,18},{3,19},{4,20},{5,21},{6,22},{7,23},{8,24},{9,... | collective-permute-start | bytes 1179656 | tf_op jit(solution)/shard_map/ppermute | solution.py:16
  (20 other events, 27.3 us)
Sparse Core Ops, SparseCore 0:
  322.0 20.4 reduce-scatter.9
  363.4 288.1 reduce-scatter.5
  657.8 170.2 reduce-scatter.7
where the time goes:
time: 847 us; the launch traced here: 835 us
  waiting for transfers between devices  437 us (52%)
  local copies, waits for them, and re-layouts  153 us (18%)
  other arithmetic  108 us (13%)
  matrix products  57 us (7%)
  blocking collectives  44.7 us (5%)
  between operations  14.6 us (2%)
  starting transfers between devices  11.5 us (1%)
  loops' own time  9.49 us (1%)
    reduce_scatter x1, waiting for transfers between devices, local(): lax.psum_scatter(in_total[None], 'rows', scatter_dimension=3, tiled=True)  205 us
    reduce_scatter x1, waiting for transfers between devices, local(): lax.psum_scatter(partial_sum, 'rows', scatter_dimension=1, tiled=True)  177 us
    unnamed x42, local copies, waits for them, and re-layouts  59.1 us
    ppermute x8, waiting for transfers between devices, passed_along(): return lax.ppermute(array, axis, pairs)  55.4 us
    psum x1, blocking collectives, local(): lax.psum((front_total, mixer_total, feed_total), ('section', 'rows'))  44.7 us
    another operation x2, other arithmetic, local(): jnp.stack([in_store[layer_index] for layer_index in range(layer_total)])  26.6 us
    another operation x3, other arithmetic, local(): jnp.stack([out_store[layer_index] for layer_index in range(layer_total)])  21.4 us
    cond x2, local copies, waits for them, and re-layouts, local(): lax.cond(own_section == sublayer, active_backward, resting_backward, (kep...  19.1 us
  transfers between devices with their start and end apart: 11, of which 9 were waited for; matrix products, arithmetic and copies ran while one was open for 10% of the time, Pallas kernels for 0%

commit v1 on v0

--- a/solution.py
+++ b/solution.py
@@ -1,13 +1,636 @@
 import jax
 import jax.numpy as jnp
 from jax import lax
+from jax.experimental import pallas as pl
+from jax.experimental.pallas import tpu as pltpu
 from jax.sharding import PartitionSpec as P
 
 HEAD_DIM = 64
 SEQ = 128
-
-
 EPSILON = 1e-05
+MESH = pl.DeviceIdType.MESH
+BF = jnp.bfloat16
+F32 = jnp.float32
+
+
+def dot(a, b, ca, cb):
+    return lax.dot_general(a, b, (((ca,), (cb,)), ((), ())), preferred_element_type=F32)
+
+
+def fold(v):
+    parts = [v[:, i : i + 128] for i in range(0, v.shape[1], 128)]
+    total = parts[0]
+    for part in parts[1:]:
+        total = total + part
+    return total
+
+
+def hat(v):
+    centered = v - jnp.mean(v, axis=-1, keepdims=True)
+    rs = lax.rsqrt(jnp.mean(centered * centered, axis=-1, keepdims=True) + EPSILON)
+    return centered * rs, rs
+
+
+def hat_back(xh, rs, dxh):
+    m1 = jnp.mean(dxh, axis=-1, keepdims=True)
+    m2 = jnp.mean(dxh * xh, axis=-1, keepdims=True)
+    return rs * (dxh - m1 - xh * m2)
+
+
+def flip(bit, by):
+    return 1 - bit if by else bit
+
+
+AX, AM, AY, FX, FY, OX, OY = range(7)
+
+
+def body(
+    tok, seg, in_hbm, out_hbm, gf, gm, gff, cot,
+    lay_o, inp_o, gi_o, go_o, gain_o,
+    W, WO, XS, YS, XR, YR, R2, R3, R4, QKV, PB, CTX, ST, UP, XH, GP, RSB, BIG, HG, QG, DC, OSND, ORCV, GS, GR,
+    wsem, wsend, wosem, isend, irecv, s2s, s2r, s3s, s3r, s4s, s4r, gss, gsr, tss, tsr,
+):
+    s = lax.axis_index("section")
+    r = lax.axis_index("rows")
+    x = lax.rem(r, 2)
+    y = lax.rem(r // 2, 2)
+    zl = lax.rem(r // 4, 2)
+    zh = r // 8
+    rx = r + 1 - 2 * x
+    ry = r + 2 - 4 * y
+    rl = r + 4 - 8 * zl
+    rh = r + 8 - 16 * zh
+    other = 1 - s
+    pending = []
+
+    def remote(src, dst, ssem, rsem, sec, row):
+        return pltpu.make_async_remote_copy(
+            src_ref=src, dst_ref=dst, send_sem=ssem, recv_sem=rsem, device_id=(sec, row), device_id_type=MESH
+        )
+
+    for l in range(2):
+        for j in range(4):
+            cols = pl.ds(768 * j, 768)
+            pltpu.make_async_copy(in_hbm.at[0, l, :, cols], W.at[s, l, :, cols], wsem.at[s, l, j]).start()
+    wo0 = pltpu.make_async_copy(out_hbm.at[0], WO, wosem.at[0])
+    wo0.start()
+
+    barrier = pltpu.get_barrier_semaphore()
+    peers = [(other, r), (0, rx), (1, rx), (0, ry), (1, ry), (0, rl), (1, rl), (s, rh)]
+    for peer in peers:
+        pl.semaphore_signal(barrier, inc=1, device_id=peer, device_id_type=MESH)
+    pl.semaphore_wait(barrier, len(peers))
+
+    for l in range(2):
+        for j in range(4):
+            cols = pl.ds(768 * j, 768)
+            cp = remote(in_hbm.at[0, l, :, cols], W.at[s, l, :, cols], wsend.at[l, j], wsem.at[s, l, j], other, r)
+            cp.start()
+            pending.append((None, cp))
+
+    def wait_w(sec, l, j):
+        cols = pl.ds(768 * j, 768)
+        pltpu.make_async_copy(in_hbm.at[0, l, :, cols], W.at[sec, l, :, cols], wsem.at[sec, l, j]).wait()
+
+    def exchange(item, l, own, far, dst, core, nb, bit, keep=None):
+        k = 2 * bit + s
+        n = 7 * l + item
+
+        def start_own():
+            @pl.when(s == core)
+            def _():
+                pltpu.make_async_copy(own, dst.at[k], irecv.at[n, k]).start()
+
+            @pl.when(s != core)
+            def _():
+                remote(own, dst.at[k], isend.at[n, 0], irecv.at[n, k], core, r).start()
+
+        def start_far():
+            remote(far, dst.at[k], isend.at[n, 1], irecv.at[n, k], core, nb).start()
+
+        cp_own = remote(own, dst.at[k], isend.at[n, 0], irecv.at[n, k], core, r)
+        cp_far = remote(far, dst.at[k], isend.at[n, 1], irecv.at[n, k], core, nb)
+        if keep is None:
+            start_far()
+            start_own()
+            pending.append((None, cp_far))
+            pending.append((s != core, cp_own))
+        else:
+            pl.when(bit == 0)(start_far)
+            pl.when(bit == 1)(start_own)
+            pending.append((bit == 0, cp_far))
+            pending.append(((bit == 1) & (s != core), cp_own))
+
+    def wait_item(n, dst):
+        for k in range(4):
+            pltpu.make_async_copy(dst.at[k], dst.at[k], irecv.at[n, k]).wait()
+
+    def x_normed(l):
+        return XS.at[l]
+
+    def x_mixer(l):
+        return XS.at[2 + l]
+
+    def x_fnormed(l):
+        return XS.at[4 + l]
+
+    def x_branch(l):
+        return XS.at[6 + l]
+
+    xr_of = (0, 1, 3)
+
+    def y_halves(ys, dim, bit):
+        if dim == 0:
+            return ys.at[:, bit], ys.at[:, 1 - bit]
+        if dim == 1:
+            return ys.at[:, :, bit], ys.at[:, :, 1 - bit]
+        return ys.at[:, :, :, bit], ys.at[:, :, :, 1 - bit]
+
+    def send_normed(l):
+        exchange(AX, l, x_normed(l), x_normed(l), XR.at[xr_of[2 - l]], 0, rl, zl)
+
+    def send_mixer(l):
+        exchange(AM, l, x_mixer(l), x_mixer(l), XR.at[xr_of[2 - l] + 1], 0, rl, zl, keep=True)
+
+    def send_ya(l):
+        own, far = y_halves(YS.at[0, l], 0, zl)
+        exchange(AY, l, own, far, YR.at[2 - l], 0, rl, zl)
+
+    def send_fnormed(l):
+        exchange(FX, l, x_fnormed(l), x_fnormed(l), XR.at[xr_of[1 - l]], 1, ry, y)
+
+    def send_yf(l):
+        own, far = y_halves(YS.at[1, l], 1, y)
+        exchange(FY, l, own, far, YR.at[1 - l], 1, ry, y)
+
+    def send_branch(l):
+        slot = 0 if l == 1 else 2
+        exchange(OX, l, x_branch(l), x_branch(l), XR.at[xr_of[slot]], 1 - l, rx, x)
+
+    def send_yo(l):
+        slot = 0 if l == 1 else 2
+        own, far = y_halves(YS.at[2, l], 2, x)
+        exchange(OY, l, own, far, YR.at[slot], 1 - l, rx, x)
+
+    def store_y(job, l, c, block):
+        turned = block.T
+        zhi, zlo, yy = c // 4, lax.rem(c // 2, 2), lax.rem(c, 2)
+        YS[job, l, zhi, zlo, yy, 0] = turned[:192]
+        YS[job, l, zhi, zlo, yy, 1] = turned[192:]
+
+    lane = lax.broadcasted_iota(jnp.int32, (1, 128), 1)
+    mk0 = jnp.where(lane < 64, 1.0, 0.0).astype(BF)
+    mk1 = jnp.where(lane < 64, 0.0, 1.0).astype(BF)
+
+    def allowed():
+        ids = jnp.broadcast_to(seg[pl.ds(s, 1), :], (128, 128))
+        row = lax.broadcasted_iota(jnp.int32, (128, 128), 0)
+        col = lax.broadcasted_iota(jnp.int32, (128, 128), 1)
+        one = jnp.logical_and(ids == ids.T, row >= col)
+        return jnp.concatenate([one, one], axis=0)
+
+    def split0(v):
+        return jnp.concatenate([v * mk0, v * mk1], axis=0)
+
+    scale = HEAD_DIM ** (-0.5)
+
+    def attention_forward(l):
+        stream = ST[2 * l]
+        xh, rs = hat(stream)
+        normed = (xh * gf[l, 0:1, :]).astype(BF)
+        XS[l] = normed
+        send_normed(l)
+        for j in range(3):
+            wait_w(0, l, j)
+            for i in range(2):
+                c = 768 * j + 384 * i
+                part = dot(XS[l], W[0, l, :, c : c + 384], 1, 0).astype(BF)
+                for p in range(3):
+                    QKV[l, c // 128 + p] = part[:, 128 * p : 128 * p + 128]
+        visible = allowed()
+
+        def pair(p):
+            q, k, v = QKV[l, p], QKV[l, 6 + p], QKV[l, 12 + p]
+            scores = dot(split0(q), k, 1, 1) * scale
+            scores = jnp.where(visible, scores, -1e30)
+            e = jnp.exp(scores - jnp.max(scores, axis=-1, keepdims=True))
+            probs = e * (1.0 / jnp.sum(e, axis=-1, keepdims=True))
+            low = probs.astype(BF)
+            PB[l, p] = low
+            both = jnp.concatenate([low[:128], low[128:]], axis=1)
+            return dot(both, split0(v), 1, 0)
+
+        for p in range(6):
+            CTX[l, :, 128 * p : 128 * p + 128] = pair(p)
+        xh, rs = hat(CTX[l])
+        XS[2 + l] = (xh * gm[l : l + 1, :]).astype(BF)
+        send_mixer(l)
+        wait_w(0, l, 3)
+        branch = dot(XS[2 + l], W[0, l, :, 2304:], 1, 0).astype(BF)
+        ST[2 * l + 1] = stream + branch.astype(F32)
+
+    def feed_forward(l):
+        stream = ST[2 * l + 1]
+        xh, rs = hat(stream)
+        XS[4 + l] = (xh * gf[l, 1:2, :]).astype(BF)
+        send_fnormed(l)
+
+        def hidden(j, total):
+            for i in range(2):
+                c = pl.ds(pl.multiple_of(768 * j + 384 * i, 384), 384)
+                h = dot(XS[4 + l], W[1, l, :, c], 1, 0)
+                phi = 0.5 + 0.5 * lax.erf(h * (0.5**0.5))
+                act = h * phi
+                BIG[:, c] = act
+                GP[l, :, c] = (phi + h * (jnp.exp(-0.5 * h * h) * 0.3989422804014327)).astype(BF)
+                total = total + fold(act)
+            return total
+
+        total = jnp.zeros((128, 128), F32)
+        for j in range(4):
+            wait_w(1, l, j)
+            total = hidden(j, total)
+        width = 3072.0
+        mu = jnp.sum(total, axis=-1, keepdims=True) / width
+
+        def spread(c, acc):
+            cen = BIG[:, pl.ds(pl.multiple_of(384 * c, 384), 384)] - mu
+            return acc + fold(cen * cen)
+
+        acc = lax.fori_loop(0, 8, spread, jnp.zeros((128, 128), F32))
+        rs = lax.rsqrt(jnp.sum(acc, axis=-1, keepdims=True) / width + EPSILON)
+        RSB[l] = jnp.broadcast_to(rs, (128, 128))
+
+        def scaled(c, carry):
+            cols = pl.ds(pl.multiple_of(384 * c, 384), 384)
+            xh = (BIG[:, cols] - mu) * rs
+            XH[l, :, cols] = xh.astype(BF)
+            inner = (xh * gff[l : l + 1, cols]).astype(BF)
+            HG[:, cols] = inner
+            store_y(2, l, c, inner)
+            return carry
+
+        lax.fori_loop(0, 8, scaled, 0)
+        send_yo(l)
+        if l == 0:
+            wo0.wait()
+        else:
+            wo1.wait()
+        for n in range(0, 768, 256):
+            branch = dot(HG[...], WO[:, n : n + 256], 1, 0).astype(BF)
+            ST[2 * l + 2, :, n : n + 256] = stream[:, n : n + 256] + branch.astype(F32)
+
+    def feed_backward(l):
+        def first(c, carry):
+            a1, a2 = carry
+            for i in range(2):
+                at = 384 * (2 * c + i)
+                cols = pl.ds(pl.multiple_of(at, 384), 384)
+                ig = dot(XS[6 + l], WO[cols, :], 1, 1)
+                xh = XH[l, :, cols].astype(F32)
+                GS[0, pl.ds(6 + 4 * l + c, 1), 384 * i : 384 * i + 384] = jnp.sum(ig * xh, axis=0, keepdims=True)
+                dxh = ig * gff[l : l + 1, cols]
+                BIG[:, cols] = dxh
+                a1 = a1 + fold(dxh)
+                a2 = a2 + fold(dxh * xh)
+            return a1, a2
+
+        zero = jnp.zeros((128, 128), F32)
+        a1, a2 = lax.fori_loop(0, 4, first, (zero, zero))
+        m1 = jnp.sum(a1, axis=-1, keepdims=True) / 3072.0
+        m2 = jnp.sum(a2, axis=-1, keepdims=True) / 3072.0
+        rs = RSB[l][:, 0:1]
+
+        def second(c, carry):
+            cols = pl.ds(pl.multiple_of(384 * c, 384), 384)
+            da = rs * (BIG[:, cols] - m1 - XH[l, :, cols].astype(F32) * m2)
+            hg = (GP[l, :, cols].astype(F32) * da).astype(BF)
+            HG[:, cols] = hg
+            store_y(1, l, c, hg)
+            return carry
+
+        lax.fori_loop(0, 8, second, 0)
+        send_yf(l)
+        for n in range(0, 768, 256):
+            BIG[:, n : n + 256] = dot(HG[...], W[1, l, n : n + 256, :], 1, 1)
+        front_back(l, 1)
+
+    def front_back(l, sub):
+        ng = BIG[:, 0:768]
+        xh, rs = hat(ST[2 * l + sub])
+        GS[0, 2 * l + sub : 2 * l + sub + 1, :] = jnp.sum(ng * xh, axis=0, keepdims=True)
+        UP[...] = UP[...] + hat_back(xh, rs, ng * gf[l, sub : sub + 1, :]).astype(BF).astype(F32)
+
+    def attention_backward(l):
+        low = UP[...].astype(BF)
+        QG[:, 2304:] = low
+        for i in range(2):
+            store_y(0, l, 6 + i, low[:, 384 * i : 384 * i + 384])
+        for n in range(0, 768, 256):
+            BIG[:, n : n + 256] = dot(low, W[0, l, n : n + 256, 2304:], 1, 1)
+        ig = BIG[:, 0:768]
+        xh, rs = hat(CTX[l])
+        GS[0, 4 + l : 5 + l, :] = jnp.sum(ig * xh, axis=0, keepdims=True)
+        dctx = hat_back(xh, rs, ig * gm[l : l + 1, :]).astype(BF)
+        for p in range(6):
+            DC[p] = dctx[:, 128 * p : 128 * p + 128]
+
+        def pair(p):
+            q, k, v = QKV[l, p], QKV[l, 6 + p], QKV[l, 12 + p]
+            probs_low = PB[l, p]
+            probs = probs_low.astype(F32)
+            dcc = split0(DC[p])
+            pg = dot(dcc, v, 1, 1)
+            ds = (probs * (pg - jnp.sum(probs * pg, axis=-1, keepdims=True))).astype(BF)
+            both = jnp.concatenate([ds[:128], ds[128:]], axis=1)
+            dq = dot(both, split0(k), 1, 0) * scale
+            dk = dot(ds, split0(q), 0, 0) * scale
+            dv = dot(probs_low, dcc, 0, 0)
+            return dq.astype(BF), dk.astype(BF), dv.astype(BF)
+
+        def group(g):
+            parts = [pair(3 * g + i) for i in range(3)]
+            for which in range(3):
+                block = jnp.concatenate([part[which] for part in parts], axis=1)
+                at = 768 * which + 384 * g
+                QG[:, at : at + 384] = block
+                store_y(0, l, 2 * which + g, block)
+
+        group(0)
+        group(1)
+        send_ya(l)
+        for n in range(0, 768, 256):
+            BIG[:, n : n + 256] = dot(QG[:, 0:2304], W[0, l, n : n + 256, 0:2304], 1, 1)
+        front_back(l, 0)
+
+    def g_at(slot, n):
+        n = n + 8 if slot == 1 else n
+        sec = 1 if slot < 2 else 0
+        return W.at[sec, 1, pl.ds(192 * (n // 4), 192), pl.ds(768 * (n % 4), 768)]
+
+    def job_wait(slot):
+        if slot == 0:
+            nx, ny = jnp.where(s == 0, 7 + OX, 7 + FX), jnp.where(s == 0, 7 + OY, 7 + FY)
+        elif slot == 1:
+            nx, ny = jnp.where(s == 0, 7 + AX, FX), jnp.where(s == 0, 7 + AY, FY)
+        else:
+            nx, ny = jnp.where(s == 0, AX, OX), jnp.where(s == 0, AY, OY)
+        wait_item(nx, XR.at[xr_of[slot]])
+        wait_item(ny, YR.at[slot])
+        if slot > 0:
+
+            @pl.when((s == 0) & (zl == 1))
+            def _():
+                wait_item(7 * (2 - slot) + AM, XR.at[xr_of[slot] + 1])
+
+    d2_row = (jnp.where(s == 0, ry, rx), rx, ry)
+    d3_row = (rl, jnp.where(s == 0, ry, rl), jnp.where(s == 0, rx, rl))
+
+    def job_index(slot, r2, r3):
+        if slot == 0:
+            return flip(zl, r3), flip(jnp.where(s == 0, y, x), r2)
+        if slot == 1:
+            return flip(jnp.where(s == 0, y, zl), r3), flip(x, r2)
+        return (
+            jnp.where(s == 0, flip(y, r2), flip(zl, r3)),
+            jnp.where(s == 0, flip(x, r3), flip(y, r2)),
+        )
+
+    def job(slot):
+        job_wait(slot)
+        for r2, r4 in ((1, 1), (1, 0), (0, 1), (0, 0)):
+            h = flip(zh, r4)
+            if slot == 0:
+                xi = 0
+            else:
+                xi = jnp.where(s == 0, zl * h, 0) + xr_of[slot]
+            rows = []
+            for r3 in (1, 0):
+                i1, i2 = job_index(slot, r2, r3)
+                rows.append(jnp.concatenate([YR[slot, k, h, i1, i2] for k in range(4)], axis=1))
+            lhs = jnp.concatenate(rows, axis=0)
+            for n in range(0, 768, 256):
+                if slot == 0:
+                    rhs = XR[0, :, :, n : n + 256]
+                else:
+                    rhs = XR[xi, :, :, n : n + 256]
+                res = dot(lhs, rhs.reshape(512, 256), 1, 0).astype(BF)
+                for q, r3 in enumerate((1, 0)):
+                    g_at(slot, 4 * r2 + 2 * r3 + r4)[:, n : n + 256] = res[192 * q : 192 * q + 192]
+            if r2 == 1:
+                for r3 in (1, 0):
+                    at = 2 * r3 + r4
+                    cp = remote(
+                        g_at(slot, 4 + at), R2.at[slot, at], s2s.at[slot, at], s2r.at[slot, at], s, d2_row[slot]
+                    )
+                    cp.start()
+                    pending.append((None, cp))
+
+    def stage2(slot):
+        for r3, r4 in ((1, 1), (1, 0), (0, 1), (0, 0)):
+            at = 2 * r3 + r4
+            pltpu.make_async_copy(R2.at[slot, at], R2.at[slot, at], s2r.at[slot, at]).wait()
+            g = g_at(slot, at)
+            g[...] = (g[...].astype(F32) + R2[slot, at].astype(F32)).astype(BF)
+            if r3 == 1:
+                cp = remote(g, R3.at[slot, r4], s3s.at[slot, r4], s3r.at[slot, r4], s, d3_row[slot])
+                cp.start()
+                pending.append((None, cp))
+
+    def stage3(slot):
+        for r4 in (1, 0):
+            pltpu.make_async_copy(R3.at[slot, r4], R3.at[slot, r4], s3r.at[slot, r4]).wait()
+            g = g_at(slot, r4)
+            g[...] = (g[...].astype(F32) + R3[slot, r4].astype(F32)).astype(BF)
+            if r4 == 1:
+                cp = remote(g, R4.at[slot], s4s.at[slot], s4r.at[slot], s, rh)
+                cp.start()
+                pending.append((None, cp))
+
+    def stage4(slot):
+        pltpu.make_async_copy(R4.at[slot], R4.at[slot], s4r.at[slot]).wait()
+        g = g_at(slot, 0)
+
+        def final(lo, hi):
+            return g[:, lo:hi].astype(F32) + R4[slot, :, lo:hi].astype(F32)
+
+        if slot == 1:
+            gi_o[1 - s] = final(0, 768)
+            return
+        core = 0 if slot == 0 else 1
+        layer = 1 if slot == 0 else 0
+
+        @pl.when(s == core)
+        def _():
+            own, away = (0, 384) if core == 0 else (384, 0)
+            OSND[...] = final(away, away + 384).astype(BF)
+            remote(OSND, ORCV, tss.at[2], tsr.at[2], other, r).start()
+            go_o[layer] = final(own, own + 384)
+
+        @pl.when(s != core)
+        def _():
+            gi_o[layer] = final(0, 768)
+
+    def o_receive():
+        cp = remote(OSND, ORCV, tss.at[2], tsr.at[2], other, r)
+        cp.wait_recv()
+        go_o[s * 0 + (1 - other)] = ORCV[...].astype(F32)
+        cp.wait_send()
+
+    def gain_stage(k):
+        to = ((other, r), (s, rx), (s, ry), (s, rl), (s, rh))[k]
+        return remote(GS.at[k], GR.at[k], gss.at[k], gsr.at[k], *to)
+
+    me = pl.ds(pl.multiple_of(s * 128, 128), 128)
+    ST[0] = tok[me, :].astype(F32)
+    XS[7] = cot[me, :]
+    UP[...] = cot[me, :].astype(F32)
+    send_branch(1)
+    GS[0, 14:16, :] = jnp.zeros((2, 768), F32)
+
+    wo1 = pltpu.make_async_copy(out_hbm.at[1], WO, wosem.at[1])
+    wo2 = pltpu.make_async_copy(out_hbm.at[0], WO, wosem.at[2])
+
+    attention_forward(0)
+    feed_forward(0)
+    wo1.start()
+    attention_forward(1)
+    feed_forward(1)
+    lay_o[me, :] = ST[4].astype(BF)
+    lay_cp = remote(lay_o.at[me, :], lay_o.at[me, :], tss.at[0], tsr.at[0], other, r)
+    lay_cp.start()
+
+    feed_backward(1)
+    wo2.start()
+    attention_backward(1)
+    job(0)
+    XS[6] = UP[...].astype(BF)
+    send_branch(0)
+    wo2.wait()
+    feed_backward(0)
+    pl.when(s == 0)(lambda: None)
+    job(1)
+    attention_backward(0)
+    inp_o[me, :] = UP[...].astype(BF)
+    inp_cp = remote(inp_o.at[me, :], inp_o.at[me, :], tss.at[1], tsr.at[1], other, r)
+    inp_cp.start()
+    gain_stage(0).start()
+    stage2(0)
+    stage3(0)
+    for k in range(2):
+        gain_stage(k).wait_recv()
+        GS[k + 1] = GS[k] + GR[k]
+        gain_stage(k + 1).start()
+    stage2(1)
+    job(2)
+    stage4(0)
+    stage3(1)
+    for k in range(2, 4):
+        gain_stage(k).wait_recv()
+        GS[k + 1] = GS[k] + GR[k]
+        gain_stage(k + 1).start()
+    stage4(1)
+    stage2(2)
+    stage3(2)
+    gain_stage(4).wait_recv()
+    gain_o[...] = GS[4] + GR[4]
+    stage4(2)
+    o_receive()
+    for k in range(5):
+        gain_stage(k).wait_send()
+    other_half = pl.ds(pl.multiple_of(other * 128, 128), 128)
+    remote(lay_o.at[other_half, :], lay_o.at[other_half, :], tss.at[0], tsr.at[0], other, r).wait_recv()
+    remote(inp_o.at[other_half, :], inp_o.at[other_half, :], tss.at[1], tsr.at[1], other, r).wait_recv()
+    lay_cp.wait_send()
+    inp_cp.wait_send()
+    for cond, cp in pending:
+        if cond is None:
+            cp.wait_send()
+        else:
+            pl.when(cond)(cp.wait_send)
+
+
+def fused(tokens, segment_ids, in_proj, out_proj, front_gain, mixer_gain, feed_gain, cotangent):
+    vm = pl.BlockSpec(memory_space=pltpu.VMEM)
+    hbm = pl.BlockSpec(memory_space=pl.ANY)
+    dma = pltpu.SemaphoreType.DMA
+    outs = pl.pallas_call(
+        body,
+        out_shape=(
+            jax.ShapeDtypeStruct((256, 768), BF),
+            jax.ShapeDtypeStruct((256, 768), BF),
+            jax.ShapeDtypeStruct((2, 192, 768), F32),
+            jax.ShapeDtypeStruct((2, 192, 384), F32),
+            jax.ShapeDtypeStruct((16, 768), F32),
+        ),
+        in_specs=[vm, vm, hbm, hbm, vm, vm, vm, vm],
+        out_specs=(vm, vm, vm, vm, vm),
+        scratch_shapes=[
+            pltpu.VMEM((2, 2, 768, 3072), BF),
+            pltpu.VMEM((3072, 768), BF),
+            pltpu.VMEM((8, 128, 768), BF),
+            pltpu.VMEM((3, 2, 2, 2, 2, 2, 192, 128), BF),
+            pltpu.VMEM((5, 4, 128, 768), BF),
+            pltpu.VMEM((3, 4, 2, 2, 2, 192, 128), BF),
+            pltpu.VMEM((3, 4, 192, 768), BF),
+            pltpu.VMEM((3, 2, 192, 768), BF),
+            pltpu.VMEM((3, 192, 768), BF),
+            pltpu.VMEM((2, 18, 128, 128), BF),
+            pltpu.VMEM((2, 6, 256, 128), BF),
+            pltpu.VMEM((2, 128, 768), F32),
+            pltpu.VMEM((5, 128, 768), F32),
+            pltpu.VMEM((128, 768), F32),
+            pltpu.VMEM((2, 128, 3072), BF),
+            pltpu.VMEM((2, 128, 3072), BF),
+            pltpu.VMEM((2, 128, 128), F32),
+            pltpu.VMEM((128, 3072), F32),
+            pltpu.VMEM((128, 3072), BF),
+            pltpu.VMEM((128, 3072), BF),
+            pltpu.VMEM((6, 128, 128), BF),
+            pltpu.VMEM((192, 384), BF),
+            pltpu.VMEM((192, 384), BF),
+            pltpu.VMEM((5, 16, 768), F32),
+            pltpu.VMEM((5, 16, 768), F32),
+            dma((2, 2, 4)),
+            dma((2, 4)),
+            dma((3,)),
+            dma((14, 2)),
+            dma((14, 4)),
+            dma((3, 4)),
+            dma((3, 4)),
+            dma((3, 2)),
+            dma((3, 2)),
+            dma((3,)),
+            dma((3,)),
+            dma((5,)),
+            dma((5,)),
+            dma((3,)),
+            dma((3,)),
+        ],
+        compiler_params=pltpu.CompilerParams(
+            collective_id=0, has_side_effects=True, vmem_limit_bytes=63 * 2**20
+        ),
+        name="layers",
+    )(
+        tokens,
+        segment_ids.reshape(2, SEQ),
+        in_proj,
+        out_proj,
+        front_gain,
+        mixer_gain,
+        feed_gain,
+        cotangent,
+    )
+    layer_out, input_grad, in_turned, out_grad, gains = outs
+    return (
+        layer_out,
+        input_grad,
+        jnp.swapaxes(in_turned, 1, 2)[None],
+        out_grad,
+        gains[0:4].reshape(2, 2, 768),
+        gains[4:6],
+        gains[6:14].reshape(2, 3072),
+    )
 
 
 def passed_along(array, axis, by):
@@ -168,7 +791,7 @@
         store[label] = value
 
 
-def local(tokens, segment_ids, in_proj, out_proj, front_gain, mixer_gain, feed_gain, cotangent):
+def generic(tokens, segment_ids, in_proj, out_proj, front_gain, mixer_gain, feed_gain, cotangent):
     own_section = lax.axis_index("section")
     own_weights = in_proj[0]
     layer_total = own_weights.shape[0]
@@ -319,6 +942,7 @@
 
 
 def solution(mesh):
+    local = fused if mesh.shape["rows"] == 16 and mesh.shape["section"] == 2 else generic
     return jax.shard_map(
         local,
         mesh=mesh,

time: 847 us -> 138 us (0.16); the launches traced: 835 us -> 137 us
  waiting for transfers between devices: 437 us -> 0 us
  local copies, waits for them, and re-layouts: 153 us -> 11.9 us
  Pallas kernels: 0 us -> 125 us
  other arithmetic: 108 us -> 0 us
  matrix products: 57 us -> 0 us
  blocking collectives: 44.7 us -> 0 us
  between operations: 14.6 us -> 0.65 us
  starting transfers between devices: 11.5 us -> 0 us
  loops' own time: 9.49 us -> 0 us
    reduce_scatter x2 -> x0, waiting for transfers between devices: 381 us -> none  [the longest x1 205 us: local(): lax.psum_scatter(in_total[None], 'rows', scatter_dimension=3, tiled=True)]
    pallas_call x0 -> x1, Pallas kernels: none -> 125 us  [fused(): pl.pallas_call(body, out_shape=(jax.ShapeDtypeStruct((256, 768), BF), jax...]
    ppermute x8 -> x0, waiting for transfers between devices: 55.4 us -> none  [passed_along(): return lax.ppermute(array, axis, pairs)]
    unnamed x42 -> x4, local copies, waits for them, and re-layouts: 59.1 us -> 7.81 us
    another operation x12 -> x0, other arithmetic: 49 us -> none  [the longest x2 26.6 us: local(): jnp.stack([in_store[layer_index] for layer_index in range(layer_total)])]
    dot_general x26 -> x0, matrix products: 47.4 us -> none  [the longest x2 9.55 us: attention_backward(): jnp.einsum('tc,td->cd', normed, projected_grad, preferred_element_type=jn...]
    psum x1 -> x0, blocking collectives: 44.7 us -> none  [local(): lax.psum((front_total, mixer_total, feed_total), ('section', 'rows'))]
    cond x80 -> x0, local copies, waits for them, and re-layouts: 30.8 us -> none  [the longest x2 19.1 us: local(): lax.cond(own_section == sublayer, active_backward, resting_backward, (kep...]
  transfers between devices with their start and end apart: 11 -> 0, of which waited for: 9 -> 0; matrix products, arithmetic and copies ran while one was open for 10% -> 0% of each run, Pallas kernels for 0% -> 0%
where the time goes in v1:
time: 138 us; the launch traced here: 137 us
  Pallas kernels  125 us (91%)
  local copies, waits for them, and re-layouts  11.9 us (9%)
    pallas_call x1, Pallas kernels, fused(): pl.pallas_call(body, out_shape=(jax.ShapeDtypeStruct((256, 768), BF), jax...  125 us
    unnamed x4, local copies, waits for them, and re-layouts  7.81 us

profile of v1, /device:TPU:0, one launch (start us, length us, event | category | flops | bytes accessed | tf_op | source)
XLA Modules:
  0.0 137.3 jit_solution(9309682641926853440)
XLA Ops:
  0.6 124.7 %layers.1 = (bf16[256,768]{1,0:T(8,128)(2,1)}, bf16[256,768]{1,0:T(8,128)(2,1)}, f32[2,192,768]{2,1,0:T(8,128)}, f32[2,192,384]{2,1,0:T(8,128)}, f32[16,768]{1,0:T(8,128)}) custom-call(bf16[256,768]{1,0:T(8,128)(2,1)} %tok.1, s32[2,128]{1,0:T(2,128)} %bitcast.5, bf16[1,2,768,3072]{3,2,1,0:T(8,128)(2,1)} %in_hbm.1, bf16[2,3072,768]{2,1,0:T(8,128)(2,1)} %out_hbm.1, ...), custom_call_target="tpu_custom_call" | custom-call | tf_op jit(solution)/shard_map/layers/pallas_call | solution.py:557
  125.3 1.3 slice.10
  126.7 0.7 slice.9
  127.4 0.8 slice.11
  128.2 0.6 reshape.25
  128.8 0.6 reshape.24
  129.5 1.8 %copy.19 = bf16[256,768]{1,0:T(8,128)(2,1)} copy(bf16[256,768]{1,0:T(8,128)(2,1)} %get-tuple-element.24) | data formatting | bytes 786432
  131.2 1.8 %copy.20 = bf16[256,768]{1,0:T(8,128)(2,1)} copy(bf16[256,768]{1,0:T(8,128)(2,1)} %get-tuple-element.25) | data formatting | bytes 786432
  133.0 2.4 %copy.21 = f32[1,2,768,192]{2,3,1,0:T(8,128)} copy(f32[1,2,768,192]{2,3,1,0:T(8,128)} %bitcast.4) | data formatting | bytes 2359296
  135.3 1.9 %copy.22 = f32[2,192,384]{2,1,0:T(8,128)} copy(f32[2,192,384]{2,1,0:T(8,128)} %get-tuple-element.27) | data formatting | bytes 1179648

commit v2 on v0

--- a/solution.py
+++ b/solution.py
@@ -1,13 +1,673 @@
 import jax
 import jax.numpy as jnp
 from jax import lax
+from jax.experimental import pallas as pl
+from jax.experimental.pallas import tpu as pltpu
 from jax.sharding import PartitionSpec as P
 
 HEAD_DIM = 64
 SEQ = 128
-
-
 EPSILON = 1e-05
+MESH = pl.DeviceIdType.MESH
+BF = jnp.bfloat16
+F32 = jnp.float32
+
+
+def dot(a, b, ca, cb):
+    return lax.dot_general(a, b, (((ca,), (cb,)), ((), ())), preferred_element_type=F32)
+
+
+def fold(v):
+    parts = [v[:, i : i + 128] for i in range(0, v.shape[1], 128)]
+    total = parts[0]
+    for part in parts[1:]:
+        total = total + part
+    return total
+
+
+def hat(v):
+    centered = v - jnp.mean(v, axis=-1, keepdims=True)
+    rs = lax.rsqrt(jnp.mean(centered * centered, axis=-1, keepdims=True) + EPSILON)
+    return centered * rs, rs
+
+
+def hat_back(xh, rs, dxh):
+    m1 = jnp.mean(dxh, axis=-1, keepdims=True)
+    m2 = jnp.mean(dxh * xh, axis=-1, keepdims=True)
+    return rs * (dxh - m1 - xh * m2)
+
+
+def flip(bit, by):
+    return 1 - bit if by else bit
+
+
+AX, AM, AY = range(3)
+
+
+def body(
+    tok, seg, in_hbm, out_hbm, gf, gm, gff, cot,
+    lay_o, inp_o, gi_o, go_o, gain_o,
+    W, WO, XS, YS, XR, YR, R2, R3, R4, FN, BG, SR, FI, FG, RC, RX, RH,
+    QKV, PB, CTX, ST, UP, XH, GP, RSB, BIG, HG, ORCV, GS, GR,
+    wsem, wsend, wosem, isend, irecv, s2s, s2r, s3s, s3r, s4s, s4r,
+    fsend, frecv, f1s, f1r, f2s, f2r, f3s, f3r, gss, gsr, tss, tsr, tksem,
+):
+    s = lax.axis_index("section")
+    r = lax.axis_index("rows")
+    x = lax.rem(r, 2)
+    y = lax.rem(r // 2, 2)
+    zl = lax.rem(r // 4, 2)
+    zh = r // 8
+    dx, dy, dl, dh = 1 - 2 * x, 2 - 4 * y, 4 - 8 * zl, 8 - 16 * zh
+    rx, ry, rl, rh, rd = r + dx, r + dy, r + dl, r + dh, r + dy + dl
+    other = 1 - s
+    pending = []
+
+    def remote(src, dst, ssem, rsem, sec, row):
+        return pltpu.make_async_remote_copy(
+            src_ref=src, dst_ref=dst, send_sem=ssem, recv_sem=rsem, device_id=(sec, row), device_id_type=MESH
+        )
+
+    me = pl.ds(pl.multiple_of(s * 128, 128), 128)
+    kf = 2 * y + zl
+    tok_in = pltpu.make_async_copy(tok.at[me, :], XS.at[0, 0], tksem.at[0])
+    cot_in = pltpu.make_async_copy(cot.at[me, :], BG.at[1, kf], tksem.at[1])
+    tok_in.start()
+    cot_in.start()
+    for l in range(2):
+        for j in range(4):
+            cols = pl.ds(768 * j, 768)
+            pltpu.make_async_copy(in_hbm.at[0, l, :, cols], W.at[s, l, :, cols], wsem.at[s, l, j]).start()
+    wo = [pltpu.make_async_copy(out_hbm.at[l], WO.at[l], wosem.at[l]) for l in range(2)]
+    wo[0].start()
+    wo[1].start()
+
+    barrier = pltpu.get_barrier_semaphore()
+    peers = [(other, r), (0, rx), (1, rx), (s, ry), (s, rl), (s, rd), (s, rh)]
+    for peer in peers:
+        pl.semaphore_signal(barrier, inc=1, device_id=peer, device_id_type=MESH)
+    pl.semaphore_wait(barrier, len(peers))
+
+    for l in range(2):
+        for j in range(4):
+            cols = pl.ds(768 * j, 768)
+            cp = remote(in_hbm.at[0, l, :, cols], W.at[s, l, :, cols], wsend.at[l, j], wsem.at[s, l, j], other, r)
+            cp.start()
+            pending.append((None, cp))
+
+    def wait_w(sec, l, j):
+        cols = pl.ds(768 * j, 768)
+        pltpu.make_async_copy(in_hbm.at[0, l, :, cols], W.at[sec, l, :, cols], wsem.at[sec, l, j]).wait()
+
+    ka = 2 * x + s
+
+    def exchange(item, l, own, far, dst):
+        @pl.when(s == 0)
+        def _():
+            pltpu.make_async_copy(own, dst.at[ka], irecv.at[l, item, ka]).start()
+
+        cp_own = remote(own, dst.at[ka], isend.at[l, item, 0], irecv.at[l, item, ka], 0, r)
+        cp_far = remote(far, dst.at[ka], isend.at[l, item, 1], irecv.at[l, item, ka], 0, rx)
+        cp_far.start()
+        pl.when(s == 1)(cp_own.start)
+        pending.append((None, cp_far))
+        pending.append((s == 1, cp_own))
+
+    def wait_item(l, item, dst):
+        for k in range(4):
+            pltpu.make_async_copy(dst.at[k], dst.at[k], irecv.at[l, item, k]).wait()
+
+    def send_normed(l):
+        exchange(AX, l, XS.at[0, l], XS.at[0, l], XR.at[l, 0])
+
+    def send_mixer(l):
+        exchange(AM, l, XS.at[1, l], XS.at[1, l], XR.at[l, 1])
+
+    def send_ya(l):
+        exchange(AY, l, YS.at[l, :, :, :, x], YS.at[l, :, :, :, 1 - x], YR.at[l])
+
+    def store_y(l, c, block):
+        turned = block.T
+        YS[l, c // 4, (c // 2) % 2, c % 2, 0] = turned[:192]
+        YS[l, c // 4, (c // 2) % 2, c % 2, 1] = turned[192:]
+
+    group = ((ry, 2 * (1 - y) + zl), (rl, 2 * y + 1 - zl), (rd, 2 * (1 - y) + 1 - zl))
+
+    def share(item, l, buf):
+        for p, (row, _) in enumerate(group):
+            cp = remote(buf.at[l, kf], buf.at[l, kf], fsend.at[l, item, p], frecv.at[l, item, kf], s, row)
+            cp.start()
+            pending.append((None, cp))
+
+    def wait_share(item, l, buf):
+        for _, k in group:
+            pltpu.make_async_copy(buf.at[l, k], buf.at[l, k], frecv.at[l, item, k]).wait()
+
+    lane = lax.broadcasted_iota(jnp.int32, (1, 128), 1)
+    mk0 = jnp.where(lane < 64, 1.0, 0.0).astype(BF)
+    mk1 = jnp.where(lane < 64, 0.0, 1.0).astype(BF)
+
+    def allowed():
+        ids = jnp.broadcast_to(seg[pl.ds(s, 1), :], (128, 128))
+        row = lax.broadcasted_iota(jnp.int32, (128, 128), 0)
+        col = lax.broadcasted_iota(jnp.int32, (128, 128), 1)
+        one = jnp.logical_and(ids == ids.T, row >= col)
+        return jnp.concatenate([one, one], axis=0)
+
+    def split0(v):
+        return jnp.concatenate([v * mk0, v * mk1], axis=0)
+
+    scale = HEAD_DIM ** (-0.5)
+    width = 3072.0
+
+    def attention_forward(l):
+        stream = ST[2 * l]
+        xh, rs = hat(stream)
+        XS[0, l] = (xh * gf[l, 0:1, :]).astype(BF)
+        send_normed(l)
+        for j in range(3):
+            wait_w(0, l, j)
+            for i in range(2):
+                c = 768 * j + 384 * i
+                part = dot(XS[0, l], W[0, l, :, c : c + 384], 1, 0).astype(BF)
+                for p in range(3):
+                    QKV[l, c // 128 + p] = part[:, 128 * p : 128 * p + 128]
+        visible = allowed()
+
+        def pair(p):
+            q, k, v = QKV[l, p], QKV[l, 6 + p], QKV[l, 12 + p]
+            scores = dot(split0(q), k, 1, 1) * scale
+            scores = jnp.where(visible, scores, -1e30)
+            e = jnp.exp(scores - jnp.max(scores, axis=-1, keepdims=True))
+            probs = e * (1.0 / jnp.sum(e, axis=-1, keepdims=True))
+            low = probs.astype(BF)
+            PB[l, p] = low
+            both = jnp.concatenate([low[:128], low[128:]], axis=1)
+            return dot(both, split0(v), 1, 0)
+
+        for p in range(6):
+            CTX[l, :, 128 * p : 128 * p + 128] = pair(p)
+        xh, rs = hat(CTX[l])
+        XS[1, l] = (xh * gm[l : l + 1, :]).astype(BF)
+        send_mixer(l)
+        wait_w(0, l, 3)
+        branch = dot(XS[1, l], W[0, l, :, 2304:], 1, 0).astype(BF)
+        ST[2 * l + 1] = stream + branch.astype(F32)
+
+    def feed_forward(l):
+        stream = ST[2 * l + 1]
+        xh, rs = hat(stream)
+        FN[l, kf] = (xh * gf[l, 1:2, :]).astype(BF)
+        share(0, l, FN)
+
+        def hidden(j, total):
+            for i in range(2):
+                c = pl.ds(pl.multiple_of(768 * j + 384 * i, 384), 384)
+                h = dot(FN[l, kf], W[1, l, :, c], 1, 0)
+                phi = 0.5 + 0.5 * lax.erf(h * (0.5**0.5))
+                act = h * phi
+                BIG[:, c] = act
+                GP[l, :, c] = (phi + h * (jnp.exp(-0.5 * h * h) * 0.3989422804014327)).astype(BF)
+                total = total + fold(act)
+            return total
+
+        total = jnp.zeros((128, 128), F32)
+        for j in range(4):
+            wait_w(1, l, j)
+            total = hidden(j, total)
+        mu = jnp.sum(total, axis=-1, keepdims=True) / width
+
+        def spread(c, acc):
+            cen = BIG[:, pl.ds(pl.multiple_of(384 * c, 384), 384)] - mu
+            return acc + fold(cen * cen)
+
+        acc = lax.fori_loop(0, 8, spread, jnp.zeros((128, 128), F32))
+        rs = lax.rsqrt(jnp.sum(acc, axis=-1, keepdims=True) / width + EPSILON)
+        RSB[l] = jnp.where(lane == 0, mu, rs)
+
+        def scaled(c, carry):
+            cols = pl.ds(pl.multiple_of(384 * c, 384), 384)
+            xh = (BIG[:, cols] - mu) * rs
+            XH[l, :, cols] = xh.astype(BF)
+            HG[:, cols] = (xh * gff[l : l + 1, cols]).astype(BF)
+            return carry
+
+        lax.fori_loop(0, 8, scaled, 0)
+        wo[l].wait()
+        for n in range(0, 768, 256):
+            branch = dot(HG[...], WO[l, :, n : n + 256], 1, 0).astype(BF)
+            out = stream[:, n : n + 256] + branch.astype(F32)
+            if l == 0:
+                ST[2, :, n : n + 256] = out
+            else:
+                lay_o[me, n : n + 256] = out.astype(BF)
+
+    def feed_backward(l):
+        def first(c, carry):
+            a1, a2 = carry
+            for i in range(2):
+                at = 384 * (2 * c + i)
+                cols = pl.ds(pl.multiple_of(at, 384), 384)
+                ig = dot(BG[l, kf], WO[l, cols, :], 1, 1)
+                xh = XH[l, :, cols].astype(F32)
+                GS[0, pl.ds(6 + 4 * l + c, 1), 384 * i : 384 * i + 384] = jnp.sum(ig * xh, axis=0, keepdims=True)
+                dxh = ig * gff[l : l + 1, cols]
+                BIG[:, cols] = dxh
+                a1 = a1 + fold(dxh)
+                a2 = a2 + fold(dxh * xh)
+            return a1, a2
+
+        zero = jnp.zeros((128, 128), F32)
+        a1, a2 = lax.fori_loop(0, 4, first, (zero, zero))
+        m1 = jnp.sum(a1, axis=-1, keepdims=True) / width
+        m2 = jnp.sum(a2, axis=-1, keepdims=True) / width
+        kept = RSB[l]
+        rs = kept[:, 1:2]
+        stats = jnp.where(lane < 2, kept, jnp.where(lane == 2, m1, m2))
+        SR[l, kf] = stats.T[0:8]
+        share(2, l, SR)
+
+        def second(c, carry):
+            cols = pl.ds(pl.multiple_of(384 * c, 384), 384)
+            da = rs * (BIG[:, cols] - m1 - XH[l, :, cols].astype(F32) * m2)
+            HG[:, cols] = (GP[l, :, cols].astype(F32) * da).astype(BF)
+            return carry
+
+        lax.fori_loop(0, 8, second, 0)
+        for n in range(0, 768, 256):
+            BIG[:, n : n + 256] = dot(HG[...], W[1, l, n : n + 256, :], 1, 1)
+        front_back(l, 1)
+
+    def front_back(l, sub):
+        ng = BIG[:, 0:768]
+        xh, rs = hat(ST[2 * l + sub])
+        GS[0, 2 * l + sub : 2 * l + sub + 1, :] = jnp.sum(ng * xh, axis=0, keepdims=True)
+        UP[...] = UP[...] + hat_back(xh, rs, ng * gf[l, sub : sub + 1, :]).astype(BF).astype(F32)
+
+    def attention_backward(l):
+        low = UP[...].astype(BF)
+        for i in range(2):
+            store_y(l, 6 + i, low[:, 384 * i : 384 * i + 384])
+        for n in range(0, 768, 256):
+            BIG[:, n : n + 256] = dot(low, W[0, l, n : n + 256, 2304:], 1, 1)
+        ig = BIG[:, 0:768]
+        xh, rs = hat(CTX[l])
+        GS[0, 4 + l : 5 + l, :] = jnp.sum(ig * xh, axis=0, keepdims=True)
+        dctx = hat_back(xh, rs, ig * gm[l : l + 1, :]).astype(BF)
+        HG[:, 2304:] = dctx
+
+        def pair(p):
+            q, k, v = QKV[l, p], QKV[l, 6 + p], QKV[l, 12 + p]
+            probs_low = PB[l, p]
+            probs = probs_low.astype(F32)
+            dcc = split0(HG[:, 2304 + 128 * p : 2432 + 128 * p])
+            pg = dot(dcc, v, 1, 1)
+            ds = (probs * (pg - jnp.sum(probs * pg, axis=-1, keepdims=True))).astype(BF)
+            both = jnp.concatenate([ds[:128], ds[128:]], axis=1)
+            dq = dot(both, split0(k), 1, 0) * scale
+            dk = dot(ds, split0(q), 0, 0) * scale
+            dv = dot(probs_low, dcc, 0, 0)
+            return dq.astype(BF), dk.astype(BF), dv.astype(BF)
+
+        for g in range(2):
+            parts = [pair(3 * g + i) for i in range(3)]
+            for which in range(3):
+                block = jnp.concatenate([part[which] for part in parts], axis=1)
+                at = 768 * which + 384 * g
+                HG[:, at : at + 384] = block
+                store_y(l, 2 * which + g, block)
+        send_ya(l)
+        for n in range(0, 768, 256):
+            BIG[:, n : n + 256] = dot(HG[:, 0:2304], W[0, l, n : n + 256, 0:2304], 1, 1)
+        front_back(l, 0)
+
+    def g_at(l, n):
+        return W.at[1 - l, 1, pl.ds(384 + 192 * (n // 4), 192), pl.ds(768 * (n % 4), 768)]
+
+    def a2_copy(l, at):
+        return remote(g_at(l, 4 + at), R2.at[l, at], s2s.at[l, at], s2r.at[l, at], 0, ry)
+
+    def a3_copy(l, r4):
+        return remote(g_at(l, 2 + r4), R3.at[l, r4], s3s.at[l, r4], s3r.at[l, r4], 0, rl)
+
+    def a4_copy(l):
+        return remote(g_at(l, 1), R4.at[l], s4s.at[l], s4r.at[l], 0, rh)
+
+    def a_job(l):
+        wait_item(l, AX, XR.at[l, 0])
+        wait_item(l, AM, XR.at[l, 1])
+        wait_item(l, AY, YR.at[l])
+        for r3, r4 in ((1, 1), (1, 0), (0, 1), (0, 0)):
+            h, low = flip(zh, r4), flip(zl, r3)
+            xi = h * low
+            rows = []
+            for r2 in (1, 0):
+                rows.append(jnp.concatenate([YR[l, k, h, low, flip(y, r2)] for k in range(4)], axis=1))
+            lhs = jnp.concatenate(rows, axis=0)
+            at = 2 * r3 + r4
+            for n in range(0, 768, 256):
+                res = dot(lhs, XR[l, xi, :, :, n : n + 256].reshape(512, 256), 1, 0).astype(BF)
+                g_at(l, 4 + at)[:, n : n + 256] = res[:192]
+                g_at(l, at)[:, n : n + 256] = res[192:]
+            a2_copy(l, at).start()
+
+    def a_stage2(l):
+        for r3, r4 in ((1, 1), (1, 0), (0, 1), (0, 0)):
+            at = 2 * r3 + r4
+            a2_copy(l, at).wait_recv()
+            g = g_at(l, at)
+            g[...] = (g[...].astype(F32) + R2[l, at].astype(F32)).astype(BF)
+            if r3 == 1:
+                a3_copy(l, r4).start()
+
+    def a_stage3(l):
+        for r4 in (1, 0):
+            a3_copy(l, r4).wait_recv()
+            g = g_at(l, r4)
+            g[...] = (g[...].astype(F32) + R3[l, r4].astype(F32)).astype(BF)
+            if r4 == 1:
+                a4_copy(l).start()
+
+    def a_stage4(l):
+        a4_copy(l).wait_recv()
+        gi_o[l] = g_at(l, 0)[...].astype(F32) + R4[l].astype(F32)
+
+    def a_sent(l):
+        for at in range(4):
+            a2_copy(l, at).wait_send()
+        for r4 in range(2):
+            a3_copy(l, r4).wait_send()
+        a4_copy(l).wait_send()
+
+    def f_at(l, which, q):
+        return W.at[1 - l, 1, pl.ds(0, 384), pl.ds(pl.multiple_of(768 * (2 * which + q), 768), 768)]
+
+    def f_half(l, q, half):
+        return f_at(l, s, q).at[pl.ds(pl.multiple_of(192 * half, 192), 192), :]
+
+    def f1_copy(l, q):
+        return remote(f_at(l, other, q), RC.at[l, q], f1s.at[l, q], f1r.at[l, q], other, r)
+
+    def f2_copy(l, q):
+        return remote(f_half(l, q, 1 - x), RX.at[l, q], f2s.at[l, q], f2r.at[l, q], s, rx)
+
+    def f3_copy(l):
+        return remote(f_half(l, 1, x), RH.at[l], f3s.at[l], f3r.at[l], s, rh)
+
+    def f_job(l):
+        wait_share(0, l, FN)
+        wait_share(1, l, BG)
+        wait_share(2, l, SR)
+
+        for q in (1, 0):
+            c = 4 * flip(zh, q) + 2 * zl + y
+            cols = pl.ds(pl.multiple_of(384 * c, 384), 384)
+
+            def source(k, carry):
+                stats = jnp.concatenate([SR[l, k]] * 16, axis=0).T
+                mu, rs, m1, m2 = (stats[:, i : i + 1] for i in range(4))
+                gain = gff[l : l + 1, cols]
+                h = dot(FN[l, k], W[1, l, :, cols], 1, 0)
+                phi = 0.5 + 0.5 * lax.erf(h * (0.5**0.5))
+                xh = (h * phi - mu) * rs
+                rows = pl.ds(pl.multiple_of(128 * k, 128), 128)
+                FI[rows, :] = (xh * gain).astype(BF)
+                ig = dot(BG[l, k], WO[l, cols, :], 1, 1)
+                da = rs * (ig * gain - m1 - xh * m2)
+                slope = phi + h * (jnp.exp(-0.5 * h * h) * 0.3989422804014327)
+                FG[rows, :] = (slope * da).astype(BF)
+                return carry
+
+            lax.fori_loop(0, 4, source, 0)
+            for which, (a, b) in enumerate(((FI, BG), (FG, FN))):
+                out = f_at(l, which, q)
+                for n in range(0, 768, 256):
+                    out[:, n : n + 256] = dot(a[...], b[l, :, :, n : n + 256].reshape(512, 256), 0, 0).astype(BF)
+            f1_copy(l, q).start()
+
+    def f_stage1(l):
+        for q in (1, 0):
+            f1_copy(l, q).wait_recv()
+            g = f_at(l, s, q)
+            g[...] = (g[...].astype(F32) + RC[l, q].astype(F32)).astype(BF)
+            f2_copy(l, q).start()
+
+    def f_stage2(l):
+        for q in (1, 0):
+            f2_copy(l, q).wait_recv()
+            g = f_half(l, q, x)
+            g[...] = (g[...].astype(F32) + RX[l, q].astype(F32)).astype(BF)
+            if q == 1:
+                f3_copy(l).start()
+
+    def o_copy(l):
+        return remote(RX.at[l, 1, :, pl.ds(0, 384)], ORCV.at[l], tss.at[2 + l], tsr.at[2 + l], other, r)
+
+    def f_stage3(l):
+        f3_copy(l).wait_recv()
+        g = f_half(l, 0, x)
+
+        def final(lo, hi):
+            return g[:, lo:hi].astype(F32) + RH[l, :, lo:hi].astype(F32)
+
+        @pl.when(s == 0)
+        def _():
+            RX[l, 1, :, 0:384] = final(384, 768).astype(BF)
+            o_copy(l).start()
+            go_o[l] = final(0, 384)
+
+        @pl.when(s == 1)
+        def _():
+            gi_o[l] = final(0, 768)
+
+    def f_sent(l):
+        for q in range(2):
+            f1_copy(l, q).wait_send()
+            f2_copy(l, q).wait_send()
+        f3_copy(l).wait_send()
+
+        @pl.when(s == 0)
+        def _():
+            o_copy(l).wait_send()
+
+    def gain_stage(k):
+        to = ((other, r), (s, rx), (s, ry), (s, rl), (s, rh))[k]
+        return remote(GS.at[k], GR.at[k], gss.at[k], gsr.at[k], *to)
+
+    def gain_step(k):
+        gain_stage(k).wait_recv()
+        if k == 4:
+            gain_o[...] = GS[4] + GR[4]
+        else:
+            GS[k + 1] = GS[k] + GR[k]
+            gain_stage(k + 1).start()
+
+    def on0(*steps):
+        @pl.when(s == 0)
+        def _():
+            for step in steps:
+                step()
+
+    cot_in.wait()
+    share(1, 1, BG)
+    UP[...] = BG[1, kf].astype(F32)
+    tok_in.wait()
+    ST[0] = XS[0, 0].astype(F32)
+    GS[0, 14:16, :] = jnp.zeros((2, 768), F32)
+
+    attention_forward(0)
+    feed_forward(0)
+    attention_forward(1)
+    feed_forward(1)
+    lay_cp = remote(lay_o.at[me, :], lay_o.at[me, :], tss.at[0], tsr.at[0], other, r)
+    lay_cp.start()
+
+    feed_backward(1)
+    attention_backward(1)
+    BG[0, kf] = UP[...].astype(BF)
+    share(1, 0, BG)
+    f_job(1)
+    on0(lambda: a_job(1))
+    f_stage1(1)
+    feed_backward(0)
+    attention_backward(0)
+    inp_o[me, :] = UP[...].astype(BF)
+    inp_cp = remote(inp_o.at[me, :], inp_o.at[me, :], tss.at[1], tsr.at[1], other, r)
+    inp_cp.start()
+    gain_stage(0).start()
+    f_stage2(1)
+    on0(lambda: a_stage2(1))
+    gain_step(0)
+    f_job(0)
+    gain_step(1)
+    on0(lambda: a_job(0))
+    f_stage1(0)
+    gain_step(2)
+    f_stage3(1)
+    on0(lambda: a_stage3(1))
+    gain_step(3)
+    gain_step(4)
+    f_stage2(0)
+    on0(lambda: a_stage4(1), lambda: a_stage2(0))
+    f_stage3(0)
+    on0(lambda: a_stage3(0), lambda: a_stage4(0))
+
+    @pl.when(s == 1)
+    def _():
+        for l in (1, 0):
+            o_copy(l).wait_recv()
+            go_o[l] = ORCV[l].astype(F32)
+
+    for l in range(2):
+        f_sent(l)
+        on0(lambda: a_sent(l))
+    for k in range(5):
+        gain_stage(k).wait_send()
+    other_half = pl.ds(pl.multiple_of(other * 128, 128), 128)
+    remote(lay_o.at[other_half, :], lay_o.at[other_half, :], tss.at[0], tsr.at[0], other, r).wait_recv()
+    remote(inp_o.at[other_half, :], inp_o.at[other_half, :], tss.at[1], tsr.at[1], other, r).wait_recv()
+    lay_cp.wait_send()
+    inp_cp.wait_send()
+    for cond, cp in pending:
+        if cond is None:
+            cp.wait_send()
+        else:
+            pl.when(cond)(cp.wait_send)
+
+
+def hand_over(lay, inp, gi, go, gains, lay_o, inp_o, gi_o, go_o, front_o, mixer_o, feed_o):
+    lay_o[...] = lay[...]
+    inp_o[...] = inp[...]
+    gi_o[...] = gi[...]
+    go_o[...] = go[...]
+    for l in range(2):
+        front_o[l] = gains[2 * l : 2 * l + 2, :]
+        for i in range(4):
+            feed_o[l : l + 1, 768 * i : 768 * i + 768] = gains[6 + 4 * l + i : 7 + 4 * l + i, :]
+    mixer_o[...] = gains[4:6, :]
+
+
+def fused(tokens, segment_ids, in_proj, out_proj, front_gain, mixer_gain, feed_gain, cotangent):
+    vm = pl.BlockSpec(memory_space=pltpu.VMEM)
+    hbm = pl.BlockSpec(memory_space=pl.ANY)
+    dma = pltpu.SemaphoreType.DMA
+    outs = pl.pallas_call(
+        body,
+        out_shape=(
+            jax.ShapeDtypeStruct((256, 768), BF),
+            jax.ShapeDtypeStruct((256, 768), BF),
+            jax.ShapeDtypeStruct((2, 192, 768), F32),
+            jax.ShapeDtypeStruct((2, 192, 384), F32),
+            jax.ShapeDtypeStruct((16, 768), F32),
+        ),
+        in_specs=[hbm, vm, hbm, hbm, vm, vm, vm, hbm],
+        out_specs=(vm, vm, vm, vm, vm),
+        scratch_shapes=[
+            pltpu.VMEM((2, 2, 768, 3072), BF),
+            pltpu.VMEM((2, 3072, 768), BF),
+            pltpu.VMEM((2, 2, 128, 768), BF),
+            pltpu.VMEM((2, 2, 2, 2, 2, 192, 128), BF),
+            pltpu.VMEM((2, 2, 4, 128, 768), BF),
+            pltpu.VMEM((2, 4, 2, 2, 2, 192, 128), BF),
+            pltpu.VMEM((2, 4, 192, 768), BF),
+            pltpu.VMEM((2, 2, 192, 768), BF),
+            pltpu.VMEM((2, 192, 768), BF),
+            pltpu.VMEM((2, 4, 128, 768), BF),
+            pltpu.VMEM((2, 4, 128, 768), BF),
+            pltpu.VMEM((2, 4, 8, 128), F32),
+            pltpu.VMEM((512, 384), BF),
+            pltpu.VMEM((512, 384), BF),
+            pltpu.VMEM((2, 2, 384, 768), BF),
+            pltpu.VMEM((2, 2, 192, 768), BF),
+            pltpu.VMEM((2, 192, 768), BF),
+            pltpu.VMEM((2, 18, 128, 128), BF),
+            pltpu.VMEM((2, 6, 256, 128), BF),
+            pltpu.VMEM((2, 128, 768), F32),
+            pltpu.VMEM((4, 128, 768), F32),
+            pltpu.VMEM((128, 768), F32),
+            pltpu.VMEM((2, 128, 3072), BF),
+            pltpu.VMEM((2, 128, 3072), BF),
+            pltpu.VMEM((2, 128, 128), F32),
+            pltpu.VMEM((128, 3072), F32),
+            pltpu.VMEM((128, 3072), BF),
+            pltpu.VMEM((2, 192, 384), BF),
+            pltpu.VMEM((5, 16, 768), F32),
+            pltpu.VMEM((5, 16, 768), F32),
+            dma((2, 2, 4)),
+            dma((2, 4)),
+            dma((2,)),
+            dma((2, 3, 2)),
+            dma((2, 3, 4)),
+            dma((2, 4)),
+            dma((2, 4)),
+            dma((2, 2)),
+            dma((2, 2)),
+            dma((2,)),
+            dma((2,)),
+            dma((2, 3, 3)),
+            dma((2, 3, 4)),
+            dma((2, 2)),
+            dma((2, 2)),
+            dma((2, 2)),
+            dma((2, 2)),
+            dma((2,)),
+            dma((2,)),
+            dma((5,)),
+            dma((5,)),
+            dma((4,)),
+            dma((4,)),
+            dma((2,)),
+        ],
+        compiler_params=pltpu.CompilerParams(
+            collective_id=0, has_side_effects=True, vmem_limit_bytes=63 * 2**20
+        ),
+        name="layers",
+    )(
+        tokens,
+        segment_ids.reshape(2, SEQ),
+        in_proj,
+        out_proj,
+        front_gain,
+        mixer_gain,
+        feed_gain,
+        cotangent,
+    )
+    layer_out, input_grad, in_turned, out_grad, front, mixer, feed = pl.pallas_call(
+        hand_over,
+        out_shape=(
+            jax.ShapeDtypeStruct((256, 768), BF),
+            jax.ShapeDtypeStruct((256, 768), BF),
+            jax.ShapeDtypeStruct((2, 192, 768), F32),
+            jax.ShapeDtypeStruct((2, 192, 384), F32),
+            jax.ShapeDtypeStruct((2, 2, 768), F32),
+            jax.ShapeDtypeStruct((2, 768), F32),
+            jax.ShapeDtypeStruct((2, 3072), F32),
+        ),
+        in_specs=[vm] * 5,
+        out_specs=(vm,) * 7,
+        name="hand_over",
+    )(*outs)
+    return layer_out, input_grad, jnp.swapaxes(in_turned, 1, 2)[None], out_grad, front, mixer, feed
 
 
 def passed_along(array, axis, by):
@@ -168,7 +828,7 @@
         store[label] = value
 
 
-def local(tokens, segment_ids, in_proj, out_proj, front_gain, mixer_gain, feed_gain, cotangent):
+def generic(tokens, segment_ids, in_proj, out_proj, front_gain, mixer_gain, feed_gain, cotangent):
     own_section = lax.axis_index("section")
     own_weights = in_proj[0]
     layer_total = own_weights.shape[0]
@@ -319,6 +979,7 @@
 
 
 def solution(mesh):
+    local = fused if mesh.shape["rows"] == 16 and mesh.shape["section"] == 2 else generic
     return jax.shard_map(
         local,
         mesh=mesh,

time: 847 us -> 113 us (0.13); the launches traced: 835 us -> 111 us
  waiting for transfers between devices: 437 us -> 0 us
  local copies, waits for them, and re-layouts: 153 us -> 0 us
  Pallas kernels: 0 us -> 111 us
  other arithmetic: 108 us -> 0 us
  matrix products: 57 us -> 0 us
  blocking collectives: 44.7 us -> 0 us
  between operations: 14.6 us -> 0.64 us
  starting transfers between devices: 11.5 us -> 0 us
  loops' own time: 9.49 us -> 0 us
    reduce_scatter x2 -> x0, waiting for transfers between devices: 381 us -> none  [the longest x1 205 us: local(): lax.psum_scatter(in_total[None], 'rows', scatter_dimension=3, tiled=True)]
    pallas_call x0 -> x2, Pallas kernels: none -> 111 us  [the longest x1 107 us: fused(): pl.pallas_call(body, out_shape=(jax.ShapeDtypeStruct((256, 768), BF), jax...]
    unnamed x42 -> x0, local copies, waits for them, and re-layouts: 59.1 us -> none
    ppermute x8 -> x0, waiting for transfers between devices: 55.4 us -> none  [passed_along(): return lax.ppermute(array, axis, pairs)]
    another operation x12 -> x0, other arithmetic: 49 us -> none  [the longest x2 26.6 us: local(): jnp.stack([in_store[layer_index] for layer_index in range(layer_total)])]
    dot_general x26 -> x0, matrix products: 47.4 us -> none  [the longest x2 9.55 us: attention_backward(): jnp.einsum('tc,td->cd', normed, projected_grad, preferred_element_type=jn...]
    psum x1 -> x0, blocking collectives: 44.7 us -> none  [local(): lax.psum((front_total, mixer_total, feed_total), ('section', 'rows'))]
    cond x80 -> x0, local copies, waits for them, and re-layouts: 30.8 us -> none  [the longest x2 19.1 us: local(): lax.cond(own_section == sublayer, active_backward, resting_backward, (kep...]
  transfers between devices with their start and end apart: 11 -> 0, of which waited for: 9 -> 0; matrix products, arithmetic and copies ran while one was open for 10% -> 0% of each run, Pallas kernels for 0% -> 0%
where the time goes in v2:
time: 113 us; the launch traced here: 111 us
  Pallas kernels  111 us (98%)
    pallas_call x1, Pallas kernels, fused(): pl.pallas_call(body, out_shape=(jax.ShapeDtypeStruct((256, 768), BF), jax...  107 us
    pallas_call x1, Pallas kernels, fused(): pl.pallas_call(hand_over, out_shape=(jax.ShapeDtypeStruct((256, 768), BF)...  3.2 us

profile of v2, /device:TPU:0, one launch (start us, length us, event | category | flops | bytes accessed | tf_op | source)
XLA Modules:
  0.0 111.2 jit_solution(3030410482413279251)
XLA Ops:
  0.6 107.3 %layers.1 = (bf16[256,768]{1,0:T(8,128)(2,1)}, bf16[256,768]{1,0:T(8,128)(2,1)}, f32[2,192,768]{2,1,0:T(8,128)}, f32[2,192,384]{2,1,0:T(8,128)}, f32[16,768]{1,0:T(8,128)}) custom-call(bf16[256,768]{1,0:T(8,128)(2,1)} %tok.1, s32[2,128]{1,0:T(2,128)} %bitcast.4, bf16[1,2,768,3072]{3,2,1,0:T(8,128)(2,1)} %in_hbm.1, bf16[2,3072,768]{2,1,0:T(8,128)(2,1)} %out_hbm.1, ...), custom_call_target="tpu_custom_call" | custom-call | tf_op jit(solution)/shard_map/layers/pallas_call | solution.py:574
  108.0 3.2 %hand_over.1 = (bf16[256,768]{1,0:T(8,128)(2,1)}, bf16[256,768]{1,0:T(8,128)(2,1)}, f32[2,192,768]{2,1,0:T(8,128)}, f32[2,192,384]{2,1,0:T(8,128)}, f32[2,2,768]...) custom-call(bf16[256,768]{1,0:T(8,128)(2,1)} %get-tuple-element.19.lay, bf16[256,768]{1,0:T(8,128)(2,1)} %get-tuple-element.20.inp, ...), custom_call_target="tpu_custom_call" | custom-call | tf_op jit(solution)/shard_map/hand_over/pallas_call | solution.py:655

commit v3 on v2

--- a/solution.py
+++ b/solution.py
@@ -47,10 +47,10 @@
 def body(
     tok, seg, in_hbm, out_hbm, gf, gm, gff, cot,
     lay_o, inp_o, gi_o, go_o, gain_o,
-    W, WO, XS, YS, XR, YR, R2, R3, R4, FN, BG, SR, FI, FG, RC, RX, RH,
-    QKV, PB, CTX, ST, UP, XH, GP, RSB, BIG, HG, ORCV, GS, GR,
+    W, WO, XS, YS, XR, YR, R2, R3, R4, FN, BG, SR, FG, RC, RX, RH,
+    QKV, PB, CTX, ST, UP, XH, GP, RSB, BIG, HG, ORCV, LB, GI, GO, GS, GR,
     wsem, wsend, wosem, isend, irecv, s2s, s2r, s3s, s3r, s4s, s4r,
-    fsend, frecv, f1s, f1r, f2s, f2r, f3s, f3r, gss, gsr, tss, tsr, tksem,
+    fsend, frecv, f1s, f1r, f2s, f2r, f3s, f3r, gss, gsr, tss, tsr, tksem, osem,
 ):
     s = lax.axis_index("section")
     r = lax.axis_index("rows")
@@ -131,17 +131,12 @@
         YS[l, c // 4, (c // 2) % 2, c % 2, 0] = turned[:192]
         YS[l, c // 4, (c // 2) % 2, c % 2, 1] = turned[192:]
 
-    group = ((ry, 2 * (1 - y) + zl), (rl, 2 * y + 1 - zl), (rd, 2 * (1 - y) + 1 - zl))
 
     def share(item, l, buf):
-        for p, (row, _) in enumerate(group):
+        for p, row in enumerate((ry, rl, rd)):
             cp = remote(buf.at[l, kf], buf.at[l, kf], fsend.at[l, item, p], frecv.at[l, item, kf], s, row)
             cp.start()
             pending.append((None, cp))
-
-    def wait_share(item, l, buf):
-        for _, k in group:
-            pltpu.make_async_copy(buf.at[l, k], buf.at[l, k], frecv.at[l, item, k]).wait()
 
     lane = lax.broadcasted_iota(jnp.int32, (1, 128), 1)
     mk0 = jnp.where(lane < 64, 1.0, 0.0).astype(BF)
@@ -240,7 +235,7 @@
             if l == 0:
                 ST[2, :, n : n + 256] = out
             else:
-                lay_o[me, n : n + 256] = out.astype(BF)
+                LB[0, :, n : n + 256] = out.astype(BF)
 
     def feed_backward(l):
         def first(c, carry):
@@ -324,11 +319,17 @@
     def g_at(l, n):
         return W.at[1 - l, 1, pl.ds(384 + 192 * (n // 4), 192), pl.ds(768 * (n % 4), 768)]
 
-    def a2_copy(l, at):
-        return remote(g_at(l, 4 + at), R2.at[l, at], s2s.at[l, at], s2r.at[l, at], 0, ry)
+    def piece(b2, b3, r4):
+        return 4 * b2 + 2 * b3 + 1 if r4 else 2 * b2 + 4 * b3
+
+    def a2_copy(l, b3, r4):
+        at = 2 * b3 + r4
+        src = g_at(l, piece(1, b3, r4))
+        return remote(src, R2.at[l, at], s2s.at[l, at], s2r.at[l, at], 0, ry if r4 else rl)
 
     def a3_copy(l, r4):
-        return remote(g_at(l, 2 + r4), R3.at[l, r4], s3s.at[l, r4], s3r.at[l, r4], 0, rl)
+        src = g_at(l, piece(0, 1, r4))
+        return remote(src, R3.at[l, r4], s3s.at[l, r4], s3r.at[l, r4], 0, rl if r4 else ry)
 
     def a4_copy(l):
         return remote(g_at(l, 1), R4.at[l], s4s.at[l], s4r.at[l], 0, rh)
@@ -337,50 +338,52 @@
         wait_item(l, AX, XR.at[l, 0])
         wait_item(l, AM, XR.at[l, 1])
         wait_item(l, AY, YR.at[l])
-        for r3, r4 in ((1, 1), (1, 0), (0, 1), (0, 0)):
+        for r4, r3 in ((1, 1), (1, 0), (0, 1), (0, 0)):
             h, low = flip(zh, r4), flip(zl, r3)
             xi = h * low
             rows = []
             for r2 in (1, 0):
                 rows.append(jnp.concatenate([YR[l, k, h, low, flip(y, r2)] for k in range(4)], axis=1))
             lhs = jnp.concatenate(rows, axis=0)
-            at = 2 * r3 + r4
             for n in range(0, 768, 256):
                 res = dot(lhs, XR[l, xi, :, :, n : n + 256].reshape(512, 256), 1, 0).astype(BF)
-                g_at(l, 4 + at)[:, n : n + 256] = res[:192]
-                g_at(l, at)[:, n : n + 256] = res[192:]
-            a2_copy(l, at).start()
-
-    def a_stage2(l):
-        for r3, r4 in ((1, 1), (1, 0), (0, 1), (0, 0)):
-            at = 2 * r3 + r4
-            a2_copy(l, at).wait_recv()
-            g = g_at(l, at)
-            g[...] = (g[...].astype(F32) + R2[l, at].astype(F32)).astype(BF)
-            if r3 == 1:
-                a3_copy(l, r4).start()
-
-    def a_stage3(l):
-        for r4 in (1, 0):
-            a3_copy(l, r4).wait_recv()
-            g = g_at(l, r4)
-            g[...] = (g[...].astype(F32) + R3[l, r4].astype(F32)).astype(BF)
+                g_at(l, 4 + 2 * r3 + r4)[:, n : n + 256] = res[:192]
+                g_at(l, 2 * r3 + r4)[:, n : n + 256] = res[192:]
             if r4 == 1:
-                a4_copy(l).start()
+                a2_copy(l, r3, 1).start()
+            elif r3 == 1:
+                a2_copy(l, 1, 0).start()
+                a2_copy(l, 0, 0).start()
+
+    def a_stage2(l, b3, r4):
+        a2_copy(l, b3, r4).wait_recv()
+        g = g_at(l, piece(0, b3, r4))
+        g[...] = (g[...].astype(F32) + R2[l, 2 * b3 + r4].astype(F32)).astype(BF)
+        if b3 == 1:
+            a3_copy(l, r4).start()
+
+    def a_stage3(l, r4):
+        a3_copy(l, r4).wait_recv()
+        g = g_at(l, r4)
+        g[...] = (g[...].astype(F32) + R3[l, r4].astype(F32)).astype(BF)
+        if r4 == 1:
+            a4_copy(l).start()
 
     def a_stage4(l):
         a4_copy(l).wait_recv()
-        gi_o[l] = g_at(l, 0)[...].astype(F32) + R4[l].astype(F32)
+        GI[l] = g_at(l, 0)[...].astype(F32) + R4[l].astype(F32)
+        gi_copy(l).start()
 
     def a_sent(l):
-        for at in range(4):
-            a2_copy(l, at).wait_send()
+        for b3 in range(2):
+            for r4 in range(2):
+                a2_copy(l, b3, r4).wait_send()
         for r4 in range(2):
             a3_copy(l, r4).wait_send()
         a4_copy(l).wait_send()
 
     def f_at(l, which, q):
-        return W.at[1 - l, 1, pl.ds(0, 384), pl.ds(pl.multiple_of(768 * (2 * which + q), 768), 768)]
+        return W.at[l, 1, pl.ds(0, 384), pl.ds(pl.multiple_of(768 * (2 * which + q), 768), 768)]
 
     def f_half(l, q, half):
         return f_at(l, s, q).at[pl.ds(pl.multiple_of(192 * half, 192), 192), :]
@@ -395,50 +398,72 @@
         return remote(f_half(l, 1, x), RH.at[l], f3s.at[l], f3r.at[l], s, rh)
 
     def f_job(l):
-        wait_share(0, l, FN)
-        wait_share(1, l, BG)
-        wait_share(2, l, SR)
-
-        for q in (1, 0):
-            c = 4 * flip(zh, q) + 2 * zl + y
-            cols = pl.ds(pl.multiple_of(384 * c, 384), 384)
-
-            def source(k, carry):
-                stats = jnp.concatenate([SR[l, k]] * 16, axis=0).T
-                mu, rs, m1, m2 = (stats[:, i : i + 1] for i in range(4))
+        def source(i, carry):
+            along_y, along_z = i // 2, lax.rem(i, 2)
+            k = 2 * (y + along_y - 2 * y * along_y) + zl + along_z - 2 * zl * along_z
+
+            @pl.when(i > 0)
+            def _():
+                for item, buf in enumerate((FN, BG, SR)):
+                    pltpu.make_async_copy(buf.at[l, k], buf.at[l, k], frecv.at[l, item, k]).wait()
+
+            stats = jnp.concatenate([SR[l, k]] * 16, axis=0).T
+            mu, rs, m1, m2 = (stats[:, n : n + 1] for n in range(4))
+            for q in (1, 0):
+                c = 4 * flip(zh, q) + 2 * zl + y
+                cols = pl.ds(pl.multiple_of(384 * c, 384), 384)
                 gain = gff[l : l + 1, cols]
                 h = dot(FN[l, k], W[1, l, :, cols], 1, 0)
                 phi = 0.5 + 0.5 * lax.erf(h * (0.5**0.5))
                 xh = (h * phi - mu) * rs
-                rows = pl.ds(pl.multiple_of(128 * k, 128), 128)
-                FI[rows, :] = (xh * gain).astype(BF)
+                to = pl.ds(pl.multiple_of(768 * k + 384 * q, 384), 384)
+                HG[:, to] = (xh * gain).astype(BF)
                 ig = dot(BG[l, k], WO[l, cols, :], 1, 1)
                 da = rs * (ig * gain - m1 - xh * m2)
                 slope = phi + h * (jnp.exp(-0.5 * h * h) * 0.3989422804014327)
-                FG[rows, :] = (slope * da).astype(BF)
-                return carry
-
-            lax.fori_loop(0, 4, source, 0)
-            for which, (a, b) in enumerate(((FI, BG), (FG, FN))):
+                FG[:, to] = (slope * da).astype(BF)
+            return carry
+
+        lax.fori_loop(0, 4, source, 0)
+        for q in (1, 0):
+            for which, (a, b) in enumerate(((HG, BG), (FG, FN))):
                 out = f_at(l, which, q)
+                lhs = jnp.concatenate([a[:, 768 * k + 384 * q : 768 * k + 384 * q + 384] for k in range(4)], axis=0)
                 for n in range(0, 768, 256):
-                    out[:, n : n + 256] = dot(a[...], b[l, :, :, n : n + 256].reshape(512, 256), 0, 0).astype(BF)
+                    out[:, n : n + 256] = dot(lhs, b[l, :, :, n : n + 256].reshape(512, 256), 0, 0).astype(BF)
             f1_copy(l, q).start()
 
-    def f_stage1(l):
-        for q in (1, 0):
-            f1_copy(l, q).wait_recv()
-            g = f_at(l, s, q)
-            g[...] = (g[...].astype(F32) + RC[l, q].astype(F32)).astype(BF)
-            f2_copy(l, q).start()
-
-    def f_stage2(l):
-        for q in (1, 0):
-            f2_copy(l, q).wait_recv()
-            g = f_half(l, q, x)
-            g[...] = (g[...].astype(F32) + RX[l, q].astype(F32)).astype(BF)
-            if q == 1:
-                f3_copy(l).start()
+    def f_stage1(l, q):
+        f1_copy(l, q).wait_recv()
+        g = f_at(l, s, q)
+        g[...] = (g[...].astype(F32) + RC[l, q].astype(F32)).astype(BF)
+        f2_copy(l, q).start()
+
+    def f_stage2(l, q):
+        f2_copy(l, q).wait_recv()
+        g = f_half(l, q, x)
+        g[...] = (g[...].astype(F32) + RX[l, q].astype(F32)).astype(BF)
+        if q == 1:
+            f3_copy(l).start()
+
+    def gi_copy(l):
+        return pltpu.make_async_copy(GI.at[l], gi_o.at[l], osem.at[l])
+
+    def go_copy(l):
+        return pltpu.make_async_copy(GO.at[l], go_o.at[l], osem.at[2 + l])
+
+    def rows_copies(n, out):
+        own = pltpu.make_async_copy(LB.at[n], out.at[me, :], osem.at[4 + n])
+        return own, remote(LB.at[n], out.at[me, :], tss.at[n], tsr.at[n], other, r)
+
+    def rows_out(n, out):
+        for copy in rows_copies(n, out):
+            copy.start()
+
+    def rows_done(n, out):
+        own, away = rows_copies(n, out)
+        own.wait()
+        away.wait()
 
     def o_copy(l):
         return remote(RX.at[l, 1, :, pl.ds(0, 384)], ORCV.at[l], tss.at[2 + l], tsr.at[2 + l], other, r)
@@ -454,11 +479,13 @@
         def _():
             RX[l, 1, :, 0:384] = final(384, 768).astype(BF)
             o_copy(l).start()
-            go_o[l] = final(0, 384)
+            GO[l] = final(0, 384)
+            go_copy(l).start()
 
         @pl.when(s == 1)
         def _():
-            gi_o[l] = final(0, 768)
+            GI[l] = final(0, 768)
+            gi_copy(l).start()
 
     def f_sent(l):
         for q in range(2):
@@ -477,7 +504,8 @@
     def gain_step(k):
         gain_stage(k).wait_recv()
         if k == 4:
-            gain_o[...] = GS[4] + GR[4]
+            GR[4] = GS[4] + GR[4]
+            pltpu.make_async_copy(GR.at[4], gain_o, osem.at[6]).start()
         else:
             GS[k + 1] = GS[k] + GR[k]
             gain_stage(k + 1).start()
@@ -499,8 +527,7 @@
     feed_forward(0)
     attention_forward(1)
     feed_forward(1)
-    lay_cp = remote(lay_o.at[me, :], lay_o.at[me, :], tss.at[0], tsr.at[0], other, r)
-    lay_cp.start()
+    rows_out(0, lay_o)
 
     feed_backward(1)
     attention_backward(1)
@@ -508,46 +535,55 @@
     share(1, 0, BG)
     f_job(1)
     on0(lambda: a_job(1))
-    f_stage1(1)
+    f_stage1(1, 1)
     feed_backward(0)
+    on0(lambda: a_stage2(1, 1, 1))
+    f_stage2(1, 1)
     attention_backward(0)
-    inp_o[me, :] = UP[...].astype(BF)
-    inp_cp = remote(inp_o.at[me, :], inp_o.at[me, :], tss.at[1], tsr.at[1], other, r)
-    inp_cp.start()
+    LB[1] = UP[...].astype(BF)
+    rows_out(1, inp_o)
+    on0(lambda: a_stage2(1, 1, 0), lambda: a_stage2(1, 0, 1))
+    f_job(0)
+    on0(lambda: a_stage3(1, 1))
+    f_stage1(0, 1)
+    f_stage1(1, 0)
+    on0(lambda: a_job(0))
     gain_stage(0).start()
-    f_stage2(1)
-    on0(lambda: a_stage2(1))
+    f_stage1(0, 0)
+    on0(lambda: a_stage2(0, 1, 1), lambda: a_stage2(1, 0, 0))
+    f_stage2(0, 1)
+    on0(lambda: a_stage2(0, 1, 0), lambda: a_stage2(0, 0, 1))
     gain_step(0)
-    f_job(0)
+    on0(lambda: a_stage3(0, 1))
+    f_stage2(0, 0)
+    f_stage2(1, 0)
+    on0(lambda: a_stage2(0, 0, 0))
     gain_step(1)
-    on0(lambda: a_job(0))
-    f_stage1(0)
+    on0(lambda: a_stage3(1, 0))
     gain_step(2)
     f_stage3(1)
-    on0(lambda: a_stage3(1))
+    f_stage3(0)
     gain_step(3)
+    on0(lambda: a_stage3(0, 0), lambda: a_stage4(1), lambda: a_stage4(0))
     gain_step(4)
-    f_stage2(0)
-    on0(lambda: a_stage4(1), lambda: a_stage2(0))
-    f_stage3(0)
-    on0(lambda: a_stage3(0), lambda: a_stage4(0))
 
     @pl.when(s == 1)
     def _():
         for l in (1, 0):
             o_copy(l).wait_recv()
-            go_o[l] = ORCV[l].astype(F32)
+            GO[l] = ORCV[l].astype(F32)
+            go_copy(l).start()
 
     for l in range(2):
         f_sent(l)
         on0(lambda: a_sent(l))
+        gi_copy(l).wait()
+        go_copy(l).wait()
     for k in range(5):
         gain_stage(k).wait_send()
-    other_half = pl.ds(pl.multiple_of(other * 128, 128), 128)
-    remote(lay_o.at[other_half, :], lay_o.at[other_half, :], tss.at[0], tsr.at[0], other, r).wait_recv()
-    remote(inp_o.at[other_half, :], inp_o.at[other_half, :], tss.at[1], tsr.at[1], other, r).wait_recv()
-    lay_cp.wait_send()
-    inp_cp.wait_send()
+    pltpu.make_async_copy(GR.at[4], gain_o, osem.at[6]).wait()
+    rows_done(0, lay_o)
+    rows_done(1, inp_o)
     for cond, cp in pending:
         if cond is None:
             cp.wait_send()
@@ -581,7 +617,7 @@
             jax.ShapeDtypeStruct((16, 768), F32),
         ),
         in_specs=[hbm, vm, hbm, hbm, vm, vm, vm, hbm],
-        out_specs=(vm, vm, vm, vm, vm),
+        out_specs=(hbm,) * 5,
         scratch_shapes=[
             pltpu.VMEM((2, 2, 768, 3072), BF),
             pltpu.VMEM((2, 3072, 768), BF),
@@ -595,8 +631,7 @@
             pltpu.VMEM((2, 4, 128, 768), BF),
             pltpu.VMEM((2, 4, 128, 768), BF),
             pltpu.VMEM((2, 4, 8, 128), F32),
-            pltpu.VMEM((512, 384), BF),
-            pltpu.VMEM((512, 384), BF),
+            pltpu.VMEM((128, 3072), BF),
             pltpu.VMEM((2, 2, 384, 768), BF),
             pltpu.VMEM((2, 2, 192, 768), BF),
             pltpu.VMEM((2, 192, 768), BF),
@@ -611,6 +646,9 @@
             pltpu.VMEM((128, 3072), F32),
             pltpu.VMEM((128, 3072), BF),
             pltpu.VMEM((2, 192, 384), BF),
+            pltpu.VMEM((2, 128, 768), BF),
+            pltpu.VMEM((2, 192, 768), F32),
+            pltpu.VMEM((2, 192, 384), F32),
             pltpu.VMEM((5, 16, 768), F32),
             pltpu.VMEM((5, 16, 768), F32),
             dma((2, 2, 4)),
@@ -637,6 +675,7 @@
             dma((4,)),
             dma((4,)),
             dma((2,)),
+            dma((7,)),
         ],
         compiler_params=pltpu.CompilerParams(
             collective_id=0, has_side_effects=True, vmem_limit_bytes=63 * 2**20

time: 113 us -> 102 us (0.903); the launches traced: 111 us -> 102 us
  Pallas kernels: 111 us -> 101 us
    pallas_call x1, Pallas kernels: 107 us -> 97.8 us  [fused(): pl.pallas_call(body, out_shape=(jax.ShapeDtypeStruct((256, 768), BF), jax...]
where the time goes in v3:
time: 102 us
  Pallas kernels  101 us (99%)
    pallas_call x1, Pallas kernels, fused(): pl.pallas_call(body, out_shape=(jax.ShapeDtypeStruct((256, 768), BF), jax...  97.8 us
    pallas_call x1, Pallas kernels, fused(): pl.pallas_call(hand_over, out_shape=(jax.ShapeDtypeStruct((256, 768), BF)...  3.2 us

profile of v3, /device:TPU:0, one launch (start us, length us, event | category | flops | bytes accessed | tf_op | source)
XLA Modules:
  0.0 101.7 jit_solution(15052908744547495972)
XLA Ops:
  0.6 97.8 %layers.1 = (bf16[256,768]{1,0:T(8,128)(2,1)}, bf16[256,768]{1,0:T(8,128)(2,1)}, f32[2,192,768]{2,1,0:T(8,128)}, f32[2,192,384]{2,1,0:T(8,128)}, f32[16,768]{1,0:T(8,128)}) custom-call(bf16[256,768]{1,0:T(8,128)(2,1)} %tok.1, s32[2,128]{1,0:T(2,128)} %bitcast.4, bf16[1,2,768,3072]{3,2,1,0:T(8,128)(2,1)} %in_hbm.1, bf16[2,3072,768]{2,1,0:T(8,128)(2,1)} %out_hbm.1, ...), custom_call_target="tpu_custom_call" | custom-call | tf_op jit(solution)/shard_map/layers/pallas_call | solution.py:610
  98.5 3.2 %hand_over.1 = (bf16[256,768]{1,0:T(8,128)(2,1)}, bf16[256,768]{1,0:T(8,128)(2,1)}, f32[2,192,768]{2,1,0:T(8,128)}, f32[2,192,384]{2,1,0:T(8,128)}, f32[2,2,768]...) custom-call(bf16[256,768]{1,0:T(8,128)(2,1)} %get-tuple-element.19.lay, bf16[256,768]{1,0:T(8,128)(2,1)} %get-tuple-element.20.inp, ...), custom_call_target="tpu_custom_call" | custom-call | tf_op jit(solution)/shard_map/hand_over/pallas_call | solution.py:694

commit v4 on v3

--- a/solution.py
+++ b/solution.py
@@ -59,7 +59,9 @@
     zl = lax.rem(r // 4, 2)
     zh = r // 8
     dx, dy, dl, dh = 1 - 2 * x, 2 - 4 * y, 4 - 8 * zl, 8 - 16 * zh
-    rx, ry, rl, rh, rd = r + dx, r + dy, r + dl, r + dh, r + dy + dl
+    rx, ry, rl, rh = r + dx, r + dy, r + dl, r + dh
+    share_bit, share_row, across_row = (zh, zl), (rh, rl), (r + dy + dh, r + dy + dl)
+    rest_bit, rest_row = (zl, zh), (rl, rh)
     other = 1 - s
     pending = []
 
@@ -69,9 +71,9 @@
         )
 
     me = pl.ds(pl.multiple_of(s * 128, 128), 128)
-    kf = 2 * y + zl
+    kf = [2 * y + bit for bit in share_bit]
     tok_in = pltpu.make_async_copy(tok.at[me, :], XS.at[0, 0], tksem.at[0])
-    cot_in = pltpu.make_async_copy(cot.at[me, :], BG.at[1, kf], tksem.at[1])
+    cot_in = pltpu.make_async_copy(cot.at[me, :], BG.at[1, kf[1]], tksem.at[1])
     tok_in.start()
     cot_in.start()
     for l in range(2):
@@ -83,7 +85,7 @@
     wo[1].start()
 
     barrier = pltpu.get_barrier_semaphore()
-    peers = [(other, r), (0, rx), (1, rx), (s, ry), (s, rl), (s, rd), (s, rh)]
+    peers = [(other, r), (0, rx), (1, rx), (s, ry), (s, rl), (s, rh), (s, across_row[0]), (s, across_row[1])]
     for peer in peers:
         pl.semaphore_signal(barrier, inc=1, device_id=peer, device_id_type=MESH)
     pl.semaphore_wait(barrier, len(peers))
@@ -133,8 +135,9 @@
 
 
     def share(item, l, buf):
-        for p, row in enumerate((ry, rl, rd)):
-            cp = remote(buf.at[l, kf], buf.at[l, kf], fsend.at[l, item, p], frecv.at[l, item, kf], s, row)
+        for p, row in enumerate((ry, share_row[l], across_row[l])):
+            own = buf.at[l, kf[l]]
+            cp = remote(own, own, fsend.at[l, item, p], frecv.at[l, item, kf[l]], s, row)
             cp.start()
             pending.append((None, cp))
 
@@ -192,13 +195,13 @@
     def feed_forward(l):
         stream = ST[2 * l + 1]
         xh, rs = hat(stream)
-        FN[l, kf] = (xh * gf[l, 1:2, :]).astype(BF)
+        FN[l, kf[l]] = (xh * gf[l, 1:2, :]).astype(BF)
         share(0, l, FN)
 
         def hidden(j, total):
             for i in range(2):
                 c = pl.ds(pl.multiple_of(768 * j + 384 * i, 384), 384)
-                h = dot(FN[l, kf], W[1, l, :, c], 1, 0)
+                h = dot(FN[l, kf[l]], W[1, l, :, c], 1, 0)
                 phi = 0.5 + 0.5 * lax.erf(h * (0.5**0.5))
                 act = h * phi
                 BIG[:, c] = act
@@ -237,13 +240,15 @@
             else:
                 LB[0, :, n : n + 256] = out.astype(BF)
 
-    def feed_backward(l):
+    held = {}
+
+    def feed_backward_0(l):
         def first(c, carry):
             a1, a2 = carry
             for i in range(2):
                 at = 384 * (2 * c + i)
                 cols = pl.ds(pl.multiple_of(at, 384), 384)
-                ig = dot(BG[l, kf], WO[l, cols, :], 1, 1)
+                ig = dot(BG[l, kf[l]], WO[l, cols, :], 1, 1)
                 xh = XH[l, :, cols].astype(F32)
                 GS[0, pl.ds(6 + 4 * l + c, 1), 384 * i : 384 * i + 384] = jnp.sum(ig * xh, axis=0, keepdims=True)
                 dxh = ig * gff[l : l + 1, cols]
@@ -259,8 +264,12 @@
         kept = RSB[l]
         rs = kept[:, 1:2]
         stats = jnp.where(lane < 2, kept, jnp.where(lane == 2, m1, m2))
-        SR[l, kf] = stats.T[0:8]
+        SR[l, kf[l]] = stats.T[0:8]
         share(2, l, SR)
+        held[l] = m1, m2, rs
+
+    def feed_backward_1(l):
+        m1, m2, rs = held[l]
 
         def second(c, carry):
             cols = pl.ds(pl.multiple_of(384 * c, 384), 384)
@@ -279,7 +288,28 @@
         GS[0, 2 * l + sub : 2 * l + sub + 1, :] = jnp.sum(ng * xh, axis=0, keepdims=True)
         UP[...] = UP[...] + hat_back(xh, rs, ng * gf[l, sub : sub + 1, :]).astype(BF).astype(F32)
 
-    def attention_backward(l):
+    def attention_pair_back(l, p):
+        q, k, v = QKV[l, p], QKV[l, 6 + p], QKV[l, 12 + p]
+        probs_low = PB[l, p]
+        probs = probs_low.astype(F32)
+        dcc = split0(HG[:, 2304 + 128 * p : 2432 + 128 * p])
+        pg = dot(dcc, v, 1, 1)
+        ds = (probs * (pg - jnp.sum(probs * pg, axis=-1, keepdims=True))).astype(BF)
+        both = jnp.concatenate([ds[:128], ds[128:]], axis=1)
+        dq = dot(both, split0(k), 1, 0) * scale
+        dk = dot(ds, split0(q), 0, 0) * scale
+        dv = dot(probs_low, dcc, 0, 0)
+        return dq.astype(BF), dk.astype(BF), dv.astype(BF)
+
+    def attention_group_back(l, g):
+        parts = [attention_pair_back(l, 3 * g + i) for i in range(3)]
+        for which in range(3):
+            block = jnp.concatenate([part[which] for part in parts], axis=1)
+            at = 768 * which + 384 * g
+            HG[:, at : at + 384] = block
+            store_y(l, 2 * which + g, block)
+
+    def attention_backward_0(l):
         low = UP[...].astype(BF)
         for i in range(2):
             store_y(l, 6 + i, low[:, 384 * i : 384 * i + 384])
@@ -290,28 +320,13 @@
         GS[0, 4 + l : 5 + l, :] = jnp.sum(ig * xh, axis=0, keepdims=True)
         dctx = hat_back(xh, rs, ig * gm[l : l + 1, :]).astype(BF)
         HG[:, 2304:] = dctx
-
-        def pair(p):
-            q, k, v = QKV[l, p], QKV[l, 6 + p], QKV[l, 12 + p]
-            probs_low = PB[l, p]
-            probs = probs_low.astype(F32)
-            dcc = split0(HG[:, 2304 + 128 * p : 2432 + 128 * p])
-            pg = dot(dcc, v, 1, 1)
-            ds = (probs * (pg - jnp.sum(probs * pg, axis=-1, keepdims=True))).astype(BF)
-            both = jnp.concatenate([ds[:128], ds[128:]], axis=1)
-            dq = dot(both, split0(k), 1, 0) * scale
-            dk = dot(ds, split0(q), 0, 0) * scale
-            dv = dot(probs_low, dcc, 0, 0)
-            return dq.astype(BF), dk.astype(BF), dv.astype(BF)
-
-        for g in range(2):
-            parts = [pair(3 * g + i) for i in range(3)]
-            for which in range(3):
-                block = jnp.concatenate([part[which] for part in parts], axis=1)
-                at = 768 * which + 384 * g
-                HG[:, at : at + 384] = block
-                store_y(l, 2 * which + g, block)
+        attention_group_back(l, 0)
+
+    def attention_backward_1(l):
+        attention_group_back(l, 1)
         send_ya(l)
+
+    def attention_backward_2(l):
         for n in range(0, 768, 256):
             BIG[:, n : n + 256] = dot(HG[:, 0:2304], W[0, l, n : n + 256, 0:2304], 1, 1)
         front_back(l, 0)
@@ -385,22 +400,31 @@
     def f_at(l, which, q):
         return W.at[l, 1, pl.ds(0, 384), pl.ds(pl.multiple_of(768 * (2 * which + q), 768), 768)]
 
-    def f_half(l, q, half):
-        return f_at(l, s, q).at[pl.ds(pl.multiple_of(192 * half, 192), 192), :]
+    def f_rows(half, chunk=None):
+        if chunk is None:
+            return pl.ds(pl.multiple_of(192 * half, 192), 192)
+        return pl.ds(pl.multiple_of(192 * half + 96 * chunk, 96), 96)
 
     def f1_copy(l, q):
         return remote(f_at(l, other, q), RC.at[l, q], f1s.at[l, q], f1r.at[l, q], other, r)
 
-    def f2_copy(l, q):
-        return remote(f_half(l, q, 1 - x), RX.at[l, q], f2s.at[l, q], f2r.at[l, q], s, rx)
-
-    def f3_copy(l):
-        return remote(f_half(l, 1, x), RH.at[l], f3s.at[l], f3r.at[l], s, rh)
+    def f_step(step):
+        return (0, None, pl.ds(0, 192)) if step == 0 else (1, step - 1, pl.ds(96 * (step - 1), 96))
+
+    def f2_copy(l, step):
+        q, chunk, rows = f_step(step)
+        src = f_at(l, s, q).at[f_rows(1 - x, chunk), :]
+        return remote(src, RX.at[l, q, rows, :], f2s.at[l, step], f2r.at[l, step], s, rx)
+
+    def f3_copy(l, chunk):
+        src = f_at(l, s, 1).at[f_rows(x, chunk), :]
+        return remote(src, RH.at[l, pl.ds(96 * chunk, 96), :], f3s.at[l, chunk], f3r.at[l, chunk], s, rest_row[l])
 
     def f_job(l):
         def source(i, carry):
             along_y, along_z = i // 2, lax.rem(i, 2)
-            k = 2 * (y + along_y - 2 * y * along_y) + zl + along_z - 2 * zl * along_z
+            bit = share_bit[l]
+            k = 2 * (y + along_y - 2 * y * along_y) + bit + along_z - 2 * bit * along_z
 
             @pl.when(i > 0)
             def _():
@@ -410,7 +434,8 @@
             stats = jnp.concatenate([SR[l, k]] * 16, axis=0).T
             mu, rs, m1, m2 = (stats[:, n : n + 1] for n in range(4))
             for q in (1, 0):
-                c = 4 * flip(zh, q) + 2 * zl + y
+                rest = flip(rest_bit[l], q)
+                c = (4 * rest + 2 * zl if l == 1 else 4 * zh + 2 * rest) + y
                 cols = pl.ds(pl.multiple_of(384 * c, 384), 384)
                 gain = gff[l : l + 1, cols]
                 h = dot(FN[l, k], W[1, l, :, cols], 1, 0)
@@ -435,16 +460,23 @@
 
     def f_stage1(l, q):
         f1_copy(l, q).wait_recv()
-        g = f_at(l, s, q)
-        g[...] = (g[...].astype(F32) + RC[l, q].astype(F32)).astype(BF)
-        f2_copy(l, q).start()
-
-    def f_stage2(l, q):
-        f2_copy(l, q).wait_recv()
-        g = f_half(l, q, x)
-        g[...] = (g[...].astype(F32) + RX[l, q].astype(F32)).astype(BF)
+        g, got = f_at(l, s, q), RC.at[l, q]
+
+        def add(rows):
+            g[rows, :] = (g[rows, :].astype(F32) + got[rows, :].astype(F32)).astype(BF)
+
+        for step in (1, 2) if q else (0,):
+            add(f_rows(1 - x, f_step(step)[1]))
+            f2_copy(l, step).start()
+        add(f_rows(x))
+
+    def f_stage2(l, step):
+        f2_copy(l, step).wait_recv()
+        q, chunk, rows = f_step(step)
+        g = f_at(l, s, q).at[f_rows(x, chunk), :]
+        g[...] = (g[...].astype(F32) + RX[l, q, rows, :].astype(F32)).astype(BF)
         if q == 1:
-            f3_copy(l).start()
+            f3_copy(l, chunk).start()
 
     def gi_copy(l):
         return pltpu.make_async_copy(GI.at[l], gi_o.at[l], osem.at[l])
@@ -469,8 +501,9 @@
         return remote(RX.at[l, 1, :, pl.ds(0, 384)], ORCV.at[l], tss.at[2 + l], tsr.at[2 + l], other, r)
 
     def f_stage3(l):
-        f3_copy(l).wait_recv()
-        g = f_half(l, 0, x)
+        f3_copy(l, 0).wait_recv()
+        f3_copy(l, 1).wait_recv()
+        g = f_at(l, s, 0).at[f_rows(x), :]
 
         def final(lo, hi):
             return g[:, lo:hi].astype(F32) + RH[l, :, lo:hi].astype(F32)
@@ -490,15 +523,16 @@
     def f_sent(l):
         for q in range(2):
             f1_copy(l, q).wait_send()
-            f2_copy(l, q).wait_send()
-        f3_copy(l).wait_send()
+            f3_copy(l, q).wait_send()
+        for step in range(3):
+            f2_copy(l, step).wait_send()
 
         @pl.when(s == 0)
         def _():
             o_copy(l).wait_send()
 
     def gain_stage(k):
-        to = ((other, r), (s, rx), (s, ry), (s, rl), (s, rh))[k]
+        to = ((other, r), (s, rl), (s, ry), (s, rh), (s, rx))[k]
         return remote(GS.at[k], GR.at[k], gss.at[k], gsr.at[k], *to)
 
     def gain_step(k):
@@ -518,7 +552,7 @@
 
     cot_in.wait()
     share(1, 1, BG)
-    UP[...] = BG[1, kf].astype(F32)
+    UP[...] = BG[1, kf[1]].astype(F32)
     tok_in.wait()
     ST[0] = XS[0, 0].astype(F32)
     GS[0, 14:16, :] = jnp.zeros((2, 768), F32)
@@ -529,43 +563,50 @@
     feed_forward(1)
     rows_out(0, lay_o)
 
-    feed_backward(1)
-    attention_backward(1)
-    BG[0, kf] = UP[...].astype(BF)
+    feed_backward_0(1)
+    feed_backward_1(1)
+    attention_backward_0(1)
+    attention_backward_1(1)
+    attention_backward_2(1)
+    BG[0, kf[0]] = UP[...].astype(BF)
     share(1, 0, BG)
     f_job(1)
+    feed_backward_0(0)
+    f_stage1(1, 1)
     on0(lambda: a_job(1))
-    f_stage1(1, 1)
-    feed_backward(0)
-    on0(lambda: a_stage2(1, 1, 1))
-    f_stage2(1, 1)
-    attention_backward(0)
+    feed_backward_1(0)
+    attention_backward_0(0)
+    attention_backward_1(0)
+    attention_backward_2(0)
     LB[1] = UP[...].astype(BF)
     rows_out(1, inp_o)
-    on0(lambda: a_stage2(1, 1, 0), lambda: a_stage2(1, 0, 1))
+    f_stage2(1, 1)
+    on0(lambda: a_stage2(1, 1, 1))
+    f_stage2(1, 2)
+    gain_stage(0).start()
+    gain_step(0)
     f_job(0)
-    on0(lambda: a_stage3(1, 1))
-    f_stage1(0, 1)
     f_stage1(1, 0)
     on0(lambda: a_job(0))
-    gain_stage(0).start()
+    gain_step(1)
+    on0(lambda: a_stage2(1, 1, 0), lambda: a_stage2(1, 0, 1))
+    f_stage1(0, 1)
+    on0(lambda: a_stage2(1, 0, 0), lambda: a_stage2(0, 1, 1), lambda: a_stage3(1, 1))
     f_stage1(0, 0)
-    on0(lambda: a_stage2(0, 1, 1), lambda: a_stage2(1, 0, 0))
+    on0(lambda: a_stage2(0, 1, 0), lambda: a_stage2(0, 0, 1), lambda: a_stage2(0, 0, 0))
+    gain_step(2)
     f_stage2(0, 1)
-    on0(lambda: a_stage2(0, 1, 0), lambda: a_stage2(0, 0, 1))
-    gain_step(0)
+    f_stage2(1, 0)
+    f_stage2(0, 2)
     on0(lambda: a_stage3(0, 1))
+    gain_step(3)
+    on0(lambda: a_stage3(0, 0), lambda: a_stage3(1, 0))
     f_stage2(0, 0)
-    f_stage2(1, 0)
-    on0(lambda: a_stage2(0, 0, 0))
-    gain_step(1)
-    on0(lambda: a_stage3(1, 0))
-    gain_step(2)
+    on0(lambda: a_stage4(1))
+    gain_step(4)
     f_stage3(1)
     f_stage3(0)
-    gain_step(3)
-    on0(lambda: a_stage3(0, 0), lambda: a_stage4(1), lambda: a_stage4(0))
-    gain_step(4)
+    on0(lambda: a_stage4(0))
 
     @pl.when(s == 1)
     def _():
@@ -666,10 +707,10 @@
             dma((2, 3, 4)),
             dma((2, 2)),
             dma((2, 2)),
+            dma((2, 3)),
+            dma((2, 3)),
             dma((2, 2)),
             dma((2, 2)),
-            dma((2,)),
-            dma((2,)),
             dma((5,)),
             dma((5,)),
             dma((4,)),

time: 102 us -> 100 us (0.980); the launches traced: 102 us -> 98.5 us
  Pallas kernels: 101 us -> 97.9 us
    pallas_call x1, Pallas kernels: 97.8 us -> 94.7 us  [fused(): pl.pallas_call(body, out_shape=(jax.ShapeDtypeStruct((256, 768), BF), jax...]
where the time goes in v4:
time: 100 us; the launch traced here: 98.5 us
  Pallas kernels  97.9 us (98%)
    pallas_call x1, Pallas kernels, fused(): pl.pallas_call(body, out_shape=(jax.ShapeDtypeStruct((256, 768), BF), jax...  94.7 us
    pallas_call x1, Pallas kernels, fused(): pl.pallas_call(hand_over, out_shape=(jax.ShapeDtypeStruct((256, 768), BF)...  3.2 us

profile of v4, /device:TPU:0, one launch (start us, length us, event | category | flops | bytes accessed | tf_op | source)
XLA Modules:
  0.0 98.5 jit_solution(10629576302556741339)
XLA Ops:
  0.6 94.7 %layers.1 = (bf16[256,768]{1,0:T(8,128)(2,1)}, bf16[256,768]{1,0:T(8,128)(2,1)}, f32[2,192,768]{2,1,0:T(8,128)}, f32[2,192,384]{2,1,0:T(8,128)}, f32[16,768]{1,0:T(8,128)}) custom-call(bf16[256,768]{1,0:T(8,128)(2,1)} %tok.1, s32[2,128]{1,0:T(2,128)} %bitcast.4, bf16[1,2,768,3072]{3,2,1,0:T(8,128)(2,1)} %in_hbm.1, bf16[2,3072,768]{2,1,0:T(8,128)(2,1)} %out_hbm.1, ...), custom_call_target="tpu_custom_call" | custom-call | tf_op jit(solution)/shard_map/layers/pallas_call | solution.py:651
  95.3 3.2 %hand_over.1 = (bf16[256,768]{1,0:T(8,128)(2,1)}, bf16[256,768]{1,0:T(8,128)(2,1)}, f32[2,192,768]{2,1,0:T(8,128)}, f32[2,192,384]{2,1,0:T(8,128)}, f32[2,2,768]...) custom-call(bf16[256,768]{1,0:T(8,128)(2,1)} %get-tuple-element.19.lay, bf16[256,768]{1,0:T(8,128)(2,1)} %get-tuple-element.20.inp, ...), custom_call_target="tpu_custom_call" | custom-call | tf_op jit(solution)/shard_map/hand_over/pallas_call | solution.py:735

commit v5 on v4

--- a/solution.py
+++ b/solution.py
@@ -386,7 +386,7 @@
 
     def a_stage4(l):
         a4_copy(l).wait_recv()
-        GI[l] = g_at(l, 0)[...].astype(F32) + R4[l].astype(F32)
+        GI[l] = (g_at(l, 0)[...].astype(F32) + R4[l].astype(F32)).astype(BF)
         gi_copy(l).start()
 
     def a_sent(l):
@@ -512,12 +512,12 @@
         def _():
             RX[l, 1, :, 0:384] = final(384, 768).astype(BF)
             o_copy(l).start()
-            GO[l] = final(0, 384)
+            GO[l] = final(0, 384).astype(BF)
             go_copy(l).start()
 
         @pl.when(s == 1)
         def _():
-            GI[l] = final(0, 768)
+            GI[l] = final(0, 768).astype(BF)
             gi_copy(l).start()
 
     def f_sent(l):
@@ -550,6 +550,14 @@
             for step in steps:
                 step()
 
+    def operands_sent():
+        for cond, cp in pending:
+            if cond is None:
+                cp.wait_send()
+            else:
+                pl.when(cond)(cp.wait_send)
+        rows_done(0, lay_o)
+
     cot_in.wait()
     share(1, 1, BG)
     UP[...] = BG[1, kf[1]].astype(F32)
@@ -571,25 +579,26 @@
     BG[0, kf[0]] = UP[...].astype(BF)
     share(1, 0, BG)
     f_job(1)
+    f_stage1(1, 1)
     feed_backward_0(0)
-    f_stage1(1, 1)
     on0(lambda: a_job(1))
     feed_backward_1(0)
+    f_stage2(1, 1)
+    f_stage2(1, 2)
     attention_backward_0(0)
     attention_backward_1(0)
     attention_backward_2(0)
     LB[1] = UP[...].astype(BF)
     rows_out(1, inp_o)
-    f_stage2(1, 1)
     on0(lambda: a_stage2(1, 1, 1))
-    f_stage2(1, 2)
     gain_stage(0).start()
     gain_step(0)
+    on0(lambda: a_stage2(1, 1, 0))
     f_job(0)
     f_stage1(1, 0)
     on0(lambda: a_job(0))
     gain_step(1)
-    on0(lambda: a_stage2(1, 1, 0), lambda: a_stage2(1, 0, 1))
+    on0(lambda: a_stage2(1, 0, 1))
     f_stage1(0, 1)
     on0(lambda: a_stage2(1, 0, 0), lambda: a_stage2(0, 1, 1), lambda: a_stage3(1, 1))
     f_stage1(0, 0)
@@ -601,6 +610,7 @@
     on0(lambda: a_stage3(0, 1))
     gain_step(3)
     on0(lambda: a_stage3(0, 0), lambda: a_stage3(1, 0))
+    operands_sent()
     f_stage2(0, 0)
     on0(lambda: a_stage4(1))
     gain_step(4)
@@ -612,8 +622,7 @@
     def _():
         for l in (1, 0):
             o_copy(l).wait_recv()
-            GO[l] = ORCV[l].astype(F32)
-            go_copy(l).start()
+            pltpu.make_async_copy(ORCV.at[l], go_o.at[l], osem.at[2 + l]).start()
 
     for l in range(2):
         f_sent(l)
@@ -623,20 +632,14 @@
     for k in range(5):
         gain_stage(k).wait_send()
     pltpu.make_async_copy(GR.at[4], gain_o, osem.at[6]).wait()
-    rows_done(0, lay_o)
     rows_done(1, inp_o)
-    for cond, cp in pending:
-        if cond is None:
-            cp.wait_send()
-        else:
-            pl.when(cond)(cp.wait_send)
 
 
 def hand_over(lay, inp, gi, go, gains, lay_o, inp_o, gi_o, go_o, front_o, mixer_o, feed_o):
     lay_o[...] = lay[...]
     inp_o[...] = inp[...]
-    gi_o[...] = gi[...]
-    go_o[...] = go[...]
+    gi_o[...] = gi[...].astype(F32)
+    go_o[...] = go[...].astype(F32)
     for l in range(2):
         front_o[l] = gains[2 * l : 2 * l + 2, :]
         for i in range(4):
@@ -653,8 +656,8 @@
         out_shape=(
             jax.ShapeDtypeStruct((256, 768), BF),
             jax.ShapeDtypeStruct((256, 768), BF),
-            jax.ShapeDtypeStruct((2, 192, 768), F32),
-            jax.ShapeDtypeStruct((2, 192, 384), F32),
+            jax.ShapeDtypeStruct((2, 192, 768), BF),
+            jax.ShapeDtypeStruct((2, 192, 384), BF),
             jax.ShapeDtypeStruct((16, 768), F32),
         ),
         in_specs=[hbm, vm, hbm, hbm, vm, vm, vm, hbm],
@@ -688,8 +691,8 @@
             pltpu.VMEM((128, 3072), BF),
             pltpu.VMEM((2, 192, 384), BF),
             pltpu.VMEM((2, 128, 768), BF),
-            pltpu.VMEM((2, 192, 768), F32),
-            pltpu.VMEM((2, 192, 384), F32),
+            pltpu.VMEM((2, 192, 768), BF),
+            pltpu.VMEM((2, 192, 384), BF),
             pltpu.VMEM((5, 16, 768), F32),
             pltpu.VMEM((5, 16, 768), F32),
             dma((2, 2, 4)),

time: 100 us -> 99.4 us (level)
  no operation moved by 1% of the time
where the time goes in v5:
time: 99.4 us; the launch traced here: 98.6 us
  Pallas kernels  98 us (99%)
    pallas_call x1, Pallas kernels, fused(): pl.pallas_call(body, out_shape=(jax.ShapeDtypeStruct((256, 768), BF), jax...  95.1 us
    pallas_call x1, Pallas kernels, fused(): pl.pallas_call(hand_over, out_shape=(jax.ShapeDtypeStruct((256, 768), BF)...  2.9 us

profile of v5, /device:TPU:0, one launch (start us, length us, event | category | flops | bytes accessed | tf_op | source)
XLA Modules:
  0.0 98.6 jit_solution(535873070629491261)
XLA Ops:
  0.6 95.1 %layers.1 = (bf16[256,768]{1,0:T(8,128)(2,1)}, bf16[256,768]{1,0:T(8,128)(2,1)}, bf16[2,192,768]{2,1,0:T(8,128)(2,1)}, bf16[2,192,384]{2,1,0:T(8,128)(2,1)}, f32[16,768]{1,0:T(8,128)}) custom-call(bf16[256,768]{1,0:T(8,128)(2,1)} %tok.1, s32[2,128]{1,0:T(2,128)} %bitcast.4, bf16[1,2,768,3072]{3,2,1,0:T(8,128)(2,1)} %in_hbm.1, bf16[2,3072,768]{2,1,0:T(8,128)(2,1)} %out_hbm.1, ...), custom_call_target="tpu_custom_call" | custom-call | tf_op jit(solution)/shard_map/layers/pallas_call | solution.py:654
  95.7 2.9 %hand_over.1 = (bf16[256,768]{1,0:T(8,128)(2,1)}, bf16[256,768]{1,0:T(8,128)(2,1)}, f32[2,192,768]{2,1,0:T(8,128)}, f32[2,192,384]{2,1,0:T(8,128)}, f32[2,2,768]...) custom-call(bf16[256,768]{1,0:T(8,128)(2,1)} %get-tuple-element.19.lay, bf16[256,768]{1,0:T(8,128)(2,1)} %get-tuple-element.20.inp, ...), custom_call_target="tpu_custom_call" | custom-call | tf_op jit(solution)/shard_map/hand_over/pallas_call | solution.py:738
